TPU v7x, 256 devices: a whole 4x4x8 slice. The times are simulated.
256 devices in a mesh: seq: 32 (over y, x, core), dp: 8 (over z).
Axes of the slice: x: 4, y: 4, z: 8, core: 2. Of those that a mesh axis runs over, the one named last changes fastest.
Arguments:
- tokens: bfloat16 [8, 8192, 2048], P('dp', 'seq'), may hold values from -6 to 6
- w_qkv: bfloat16 [2048, 3, 1024], P('seq'), may hold values from -0.125 to 0.125
- weight_table: float32 [16, 8], replicated, may hold values from 0.3 to 3
- weight_index: int32 [8, 64, 6], P('dp', 'seq'), may hold values from 0 to 15
- cotangent: bfloat16 [8, 8192, 1024], P('dp', 'seq'), may hold values from -6 to 6
Outputs:
- attn_out: bfloat16 [8, 8192, 1024], P('dp', 'seq')
- grad_w: float32 [2048, 3, 1024], P('seq')
All inputs are finite; a program needn't handle non-finite values.
Results may differ from a plain program's by a relative error of at most 0.02.
Values may be sent and summed in bfloat16 or wider, within the bound.
No kernel may reach another device: no remote copies, remote signals or barrier semaphores. Data moves between devices by JAX's collectives and lax.ppermute only.
A program may use at most 128 MiB of HBM per device.

v0:
```python
import math

import jax
import jax.numpy as jnp
from jax import lax
from jax.experimental import pallas as pl
from jax.experimental.pallas import tpu as pltpu
from jax.sharding import Mesh, PartitionSpec as P

BF = jnp.bfloat16
F32 = jnp.float32
HEAD = 128
QB = 128
BLOCK = 256
D = 2048
COLS = 768
MIB = 1024 * 1024
SETS = 0x66
HALVES = 0xB4


def ring(value, phase, step):
    pairs = []
    for y in range(4):
        for x in range(4):
            for core in range(2):
                at = (y, (x - step) % 4) if core == phase else ((y - step) % 4, x)
                pairs.append(((y * 4 + x) * 2 + core, (at[0] * 4 + at[1]) * 2 + core))
    return lax.ppermute(value, ("y", "x", "core"), pairs)


def swap(value, axis, size, mask):
    return lax.ppermute(value, axis, [(i, i ^ mask) for i in range(size)])


def same_set_neighbour(value):
    return lax.ppermute(value, "dp", [(z, (z + 1 if z % 2 else z - 1) % 8) for z in range(8)])


def same_set_far(value):
    return lax.ppermute(value, "dp", [(z, ((7 if SETS >> z & 1 else 3) - z) % 8) for z in range(8)])


def after(value, *others):
    return lax.optimization_barrier((value, *others))[0]


def dot(a, b, ca, cb):
    return lax.dot_general(a, b, (((ca,), (cb,)), ((), ())), preferred_element_type=F32)


def smem():
    return pl.BlockSpec(memory_space=pltpu.SMEM)


def vmem():
    return pl.BlockSpec(memory_space=pltpu.VMEM)


def call(kernel, args, n_smem, outs, scratch=(), grant=16, flops=0, nbytes=0):
    return pl.pallas_call(
        kernel,
        out_shape=[jax.ShapeDtypeStruct(*out) for out in outs],
        in_specs=[smem()] * n_smem + [vmem()] * (len(args) - n_smem),
        out_specs=[vmem()] * len(outs),
        scratch_shapes=list(scratch),
        compiler_params=pltpu.CompilerParams(vmem_limit_bytes=grant * MIB),
        cost_estimate=pl.CostEstimate(flops=flops, bytes_accessed=nbytes, transcendentals=0),
    )(*args)


def lanes(start):
    return pl.ds(pl.multiple_of(start, HEAD), HEAD)


def level_coef(pos, idx, table, blk, group, level, head):
    cs = blk // 2
    y, x, core = pos[0], pos[1], pos[2]
    row = idx[blk, group * 6 + level]
    lam = table[row, (core * 2 + pos[4]) * 2 + head]
    if level == 0:
        return lam * (1.0 / math.sqrt(HEAD * BLOCK))
    bit = [(core + cs) & 1, x & 1, (x >> 1) & 1, y & 1, (y >> 1) & 1][level - 1]
    return lam * bit.astype(F32) * (1.0 / math.sqrt(HEAD * 2 ** (level - 1) * BLOCK))


def prepare_kernel(pos, w, w_own, w_core):
    core, kind = pos[2], pos[4]
    mine = pl.multiple_of((core * 2 + kind) * 256, 256)
    other = pl.multiple_of(((1 - core) * 2 + kind) * 256, 256)
    for third in range(3):
        at = slice(third * 256, third * 256 + 256)
        w_own[:, at] = w[third, :, pl.ds(mine, 256)]
        w_core[:, at] = w[third, :, pl.ds(other, 256)]


def split_kernel(pos, cot, c_own, c_z):
    core, kind = pos[2], pos[4]
    for cs in range(2):
        for zs, out in enumerate((c_own, c_z)):
            group = ((core + cs) & 1) * 2 + ((kind + zs) & 1)
            out[cs] = cot[:, pl.ds(pl.multiple_of(group * 256, 256), 256)]


def project_kernel(pos, idx, table, *refs):
    toks = refs[0:4]
    c_own, c_z, c_core = refs[4:7]
    mine, ahead, behind, far_low, far_high = refs[7:12]
    qkv, cots, s1, x0, g1, m2, m3, m4, m5, w = refs[12:]
    y, x, core = pos[0], pos[1], pos[2]

    def place(part, first, slot, dist):
        yy = (y + dist + core * (slot - dist)) & 3
        xx = (x + slot + core * (dist - slot)) & 3
        for cs in range(2):
            row = pl.multiple_of((yy * 4 + xx) * 128 + ((core + cs) & 1) * 64, 64)
            w[pl.ds(row, 64), :] = part[first + cs * 64 : first + cs * 64 + 64, :]

    for slot in range(4):
        place(mine, slot * 128, slot, 0)
        place(ahead, slot * 128, slot, 1)
        place(behind, slot * 128, slot, 3)
        place((far_low, far_high)[slot // 2], (slot % 2) * 128, slot, 2)
    cots[0] = c_own[0]
    cots[1] = c_z[0]
    cots[2] = c_core[0]
    cots[3] = c_core[1]

    @pl.loop(0, 3)
    def _(part):
        cols = pl.ds(pl.multiple_of(part * 256, 256), 256)
        for blk in range(4):
            qkv[blk, :, cols] = dot(toks[blk][...], w[:, cols], 1, 0).astype(BF)

    @pl.loop(0, 4)
    def _(step):
        zs, h = step // 2, step % 2
        total = None
        sums = [None] * 4
        for cs in range(2):
            blk = cs * 2 + zs
            state = dot(qkv[blk, :, lanes(256 + h * HEAD)], qkv[blk, :, lanes(512 + h * HEAD)], 0, 0)
            s1[blk, h] = state.astype(BF)
            total = state if total is None else total + state
            first = None
            for g in range(2):
                rows = slice(g * QB, g * QB + QB)
                outer = dot(qkv[blk, rows, lanes(h * HEAD)], cots[blk, rows, lanes(h * HEAD)], 0, 0)
                term = outer * level_coef(pos, idx, table, cs * 2 + zs, g, 1, h)
                first = term if first is None else first + term
                for k in range(4):
                    term = outer * level_coef(pos, idx, table, blk, g, k + 2, h)
                    sums[k] = term if sums[k] is None else sums[k] + term
            g1[blk, h] = first
        x0[zs, h] = total.astype(BF)
        m2[zs, h] = sums[0]
        m3[zs, h] = sums[1]
        m4[zs, h] = sums[2].astype(BF)
        m5[zs, h] = sums[3].astype(BF)


def local_kernel(pos, idx, table, qkv, cots, loc):
    rows = lax.broadcasted_iota(jnp.int32, (BLOCK, BLOCK), 0)
    cols = lax.broadcasted_iota(jnp.int32, (BLOCK, BLOCK), 1)
    causal = rows >= cols
    upper = rows < QB

    @pl.loop(0, 8)
    def _(step):
        blk, h = step // 2, step % 2
        q = qkv[blk, :, lanes(h * HEAD)]
        k = qkv[blk, :, lanes(256 + h * HEAD)]
        v = qkv[blk, :, lanes(512 + h * HEAD)]
        c = cots[blk, :, lanes(h * HEAD)]
        scale = jnp.where(
            upper,
            level_coef(pos, idx, table, blk, 0, 0, h),
            level_coef(pos, idx, table, blk, 1, 0, h),
        )
        scale = jnp.where(causal, scale, 0.0)
        scores = (dot(q, k, 1, 1) * scale).astype(BF)
        dscores = (dot(c, v, 1, 1) * scale).astype(BF)
        loc[blk, :, lanes(h * HEAD)] = dot(dscores, k, 1, 0)
        loc[blk, :, lanes(256 + h * HEAD)] = dot(dscores, q, 0, 0)
        loc[blk, :, lanes(512 + h * HEAD)] = dot(scores, c, 0, 0)
        loc[blk, :, lanes(768 + h * HEAD)] = dot(scores, v, 1, 0)


def gradient_pair(pos, toks, grads, dist, first, store):
    y, x, core, half = pos[0], pos[1], pos[2], pos[5]
    at = []
    for slot in (first, first + 1):
        yy = (y + dist + core * (slot - dist)) & 3
        xx = (x + slot + core * (dist - slot)) & 3
        at.append(lanes((yy * 4 + xx) * 128))
    part = None
    for blk in range(4):
        rows = jnp.concatenate([toks[blk][:, at[0]], toks[blk][:, at[1]]], axis=1)
        term = dot(rows, grads[blk], 0, 0)
        part = term if part is None else part + term
    part = part.astype(BF)
    for sub in range(2):
        for c in range(2):
            for piece in range(2):
                row = ((c + core) & 1) * 64 + ((piece + half) & 1) * 32
                start = sub * 128 + c * 64 + piece * 32
                store(sub, pl.ds(pl.multiple_of(row, 32), 32), part[start : start + 32])


def finish_kernel(pos, idx, table, *refs):
    toks = refs[0:4]
    cots, qkv, loc, s1, g1 = refs[4:9]
    cx1, cx2, cx3, cy1, cy2, cy3 = refs[9:15]
    own, r1, r2, r3 = refs[15:19]
    attn, grads, low, high = refs[19:]

    @pl.loop(0, 4)
    def _(step):
        zs, h = step // 2, step % 2
        far = [
            None,
            cx1[zs, h].astype(F32),
            cx2[zs, h].astype(F32) + cx3[zs, h].astype(F32),
            cy1[zs, h].astype(F32),
            cy2[zs, h].astype(F32) + cy3[zs, h].astype(F32),
        ]
        chip = own[zs, h].astype(F32) + r1[zs, h].astype(F32)
        chip = chip + r2[zs, h].astype(F32) + r3[zs, h].astype(F32)
        qs, ks = lanes(h * HEAD), lanes(256 + h * HEAD)
        vs, ats = lanes(512 + h * HEAD), lanes(768 + h * HEAD)
        for cs in range(2):
            blk = cs * 2 + zs
            other = (1 - cs) * 2 + zs
            far[0] = s1[other, h].astype(F32)
            grad = (chip + g1[other, h]).astype(BF)
            for g in range(2):
                rows = slice(g * QB, g * QB + QB)
                mixed = None
                for level in range(1, 6):
                    term = far[level - 1] * level_coef(pos, idx, table, blk, g, level, h)
                    mixed = term if mixed is None else mixed + term
                mixed = mixed.astype(BF)
                out = loc[blk, rows, ats] + dot(qkv[blk, rows, qs], mixed, 1, 0)
                attn[blk, rows, qs] = out.astype(BF)
                dq = loc[blk, rows, qs] + dot(cots[blk, rows, qs], mixed, 1, 1)
                grads[blk, rows, qs] = dq.astype(BF)
            dk = loc[blk, :, ks] + dot(qkv[blk, :, vs], grad, 1, 1)
            grads[blk, :, ks] = dk.astype(BF)
            dv = loc[blk, :, vs] + dot(qkv[blk, :, ks], grad, 1, 0)
            grads[blk, :, vs] = dv.astype(BF)

    for first, out in ((0, low), (2, high)):

        def store(sub, rows, value, out=out):
            out[sub, rows, :] = value

        gradient_pair(pos, toks, grads, 2, first, store)


def gradient_kernel(pos, t0, t1, t2, t3, grads, own, onward, backward):
    toks = (t0, t1, t2, t3)

    @pl.loop(0, 2)
    def _(pair):
        for dist, out in ((1, onward), (3, backward), (0, own)):

            def store(sub, rows, value, out=out):
                out[pair * 2 + sub, rows, :] = value

            gradient_pair(pos, toks, grads, dist, pair * 2, store)


def place_kernel(pos, own, from_core, from_z, mine, near, theirs, attn_out, grad_w):
    core, kind = pos[2], pos[4]
    attns = ((own, from_z.at[0]), (from_core.at[0], from_z.at[1]))
    halves = (pos[5], pos[6])
    for cs in range(2):
        for zs in range(2):
            group = ((core + cs) & 1) * 2 + ((kind + zs) & 1)
            lane = pl.ds(pl.multiple_of(group * 256, 256), 256)
            attn_out[:, lane] = attns[cs][zs][0] if zs == 0 and cs == 0 else attns[cs][zs][...]
            for piece in range(2):
                part = (mine, near)[piece] if zs == 0 else theirs.at[piece]
                row = pl.ds(pl.multiple_of(((halves[zs] + piece) & 1) * 32, 32), 32)
                for third in range(3):
                    grad_w[third, row, lane] = part[
                        cs, :, third * 256 : third * 256 + 256
                    ].astype(F32)


def add(*parts):
    total = parts[0].astype(F32)
    for part in parts[1:]:
        total = total + part.astype(F32)
    return total.astype(BF)


def per_device(tokens, w_qkv, weight_table, weight_index, cotangent):
    y, x, core = lax.axis_index("y"), lax.axis_index("x"), lax.axis_index("core")
    z = lax.axis_index("dp")
    pos = jnp.stack(
        [y, x, core, z, (SETS >> z) & 1, (HALVES >> z) & 1, (HALVES >> (z ^ 1)) & 1]
    ).astype(jnp.int32)
    inputs = tokens[0]

    rows = weight_index.reshape(1, 12)
    rows = jnp.concatenate([rows, swap(rows, "dp", 8, 1)], axis=0)
    idx = jnp.concatenate([rows, swap(rows, "core", 2, 1)], axis=0)
    scalars = [pos, idx, weight_table]

    w_own, w_core = call(
        prepare_kernel,
        [pos, jnp.transpose(w_qkv, (1, 0, 2))],
        1,
        [((64, COLS), BF), ((64, COLS), BF)],
        grant=48,
        nbytes=MIB,
    )

    chunk = jnp.concatenate([w_own, swap(w_core, "core", 2, 1)], axis=0)
    mine = jnp.concatenate([chunk] + [ring(chunk, 0, step) for step in (1, 2, 3)], axis=0)
    ahead, behind = ring(mine, 1, 1), ring(mine, 1, 3)
    far_low, far_high = ring(behind[:256], 1, 3), ring(ahead[256:], 1, 1)

    tok01 = swap(inputs, "dp", 8, 1)
    c_own, c_z = call(
        split_kernel,
        [pos, after(cotangent[0], chunk)],
        1,
        [((2, BLOCK, 256), BF), ((2, BLOCK, 256), BF)],
        grant=48,
        nbytes=MIB,
    )
    from_z = swap(c_z, "dp", 8, 1)
    tok10 = swap(after(inputs, mine), "core", 2, 1)
    tok11 = swap(after(tok01, behind), "core", 2, 1)
    to_core = jnp.stack([c_own[1], after(from_z, behind)[1]], axis=0)
    c_core = swap(to_core, "core", 2, 1)
    toks = [inputs, tok01, tok10, tok11]

    square = (2, 2, HEAD, HEAD)
    wide = (4, 2, HEAD, HEAD)
    qkv, cots, s1, x0, g1, m2, m3, m4, m5 = call(
        project_kernel,
        scalars + toks + [c_own, from_z, c_core, mine, ahead, behind, far_low, far_high],
        3,
        [
            ((4, BLOCK, COLS), BF),
            ((4, BLOCK, 256), BF),
            (wide, BF),
            (square, BF),
            (wide, F32),
            (square, F32),
            (square, F32),
            (square, BF),
            (square, BF),
        ],
        scratch=[pltpu.VMEM((D, COLS), BF)],
        grant=48,
        flops=2 * 1024 * D * COLS,
        nbytes=10 * MIB,
    )

    cx = [swap(x0, "x", 4, mask) for mask in (1, 2, 3)]
    dy = [swap(m, "y", 4, mask) for mask, m in ((1, m4), (2, m5), (3, m5))]
    (loc,) = call(
        local_kernel,
        scalars + [qkv, cots],
        3,
        [((4, BLOCK, 1024), F32)],
        grant=12,
        flops=8 * 6 * 2 * BLOCK * BLOCK * HEAD,
        nbytes=8 * MIB,
    )
    x1 = add(x0, *cx)
    cy = [swap(x1, "y", 4, mask) for mask in (1, 2, 3)]
    high = dy[0].astype(F32) + dy[1].astype(F32) + dy[2].astype(F32)
    near = (high + m2).astype(BF)
    far = (high + m3).astype(BF)
    dx = [swap(m, "x", 4, mask) for mask, m in ((1, near), (2, far), (3, far))]

    attn, grads, low, high = call(
        finish_kernel,
        scalars + toks + [cots, qkv, loc, s1, g1] + cx + cy + [high.astype(BF)] + dx,
        3,
        [
            ((4, BLOCK, 256), BF),
            ((4, BLOCK, COLS), BF),
            ((2, 128, COLS), BF),
            ((2, 128, COLS), BF),
        ],
        grant=24,
        flops=1024 * D * COLS,
        nbytes=12 * MIB,
    )
    low, high = ring(low, 1, 3), ring(high, 1, 1)
    own, onward, backward = call(
        gradient_kernel,
        [pos] + toks + [grads],
        1,
        [((4, 128, COLS), BF)] * 3,
        grant=24,
        flops=2 * 1024 * D * COLS,
        nbytes=9 * MIB,
    )
    onward = jnp.concatenate([add(onward[:2], low), onward[2:]], axis=0)
    backward = jnp.concatenate([backward[:2], add(backward[2:], high)], axis=0)
    from_core = swap(attn[2:], "core", 2, 1)
    total = add(own, ring(onward, 1, 3), ring(backward, 1, 1))
    back = swap(jnp.stack([attn[1], from_core[1]], axis=0), "dp", 8, 1)
    chip_sum = add(total[0], *[ring(total[step], 0, -step) for step in (1, 2, 3)])
    pair = jnp.stack([chip_sum[:64], swap(chip_sum[64:], "core", 2, 1)], axis=0)
    mine = add(pair[:, :32], same_set_neighbour(pair[:, 32:]))
    mine = add(mine, same_set_far(mine))
    near = same_set_neighbour(mine)
    theirs = swap(jnp.stack([mine, near], axis=0), "dp", 8, 1)

    attn_out, grad_w = call(
        place_kernel,
        [pos, attn, from_core, back, mine, near, theirs],
        1,
        [((BLOCK, 1024), BF), ((3, 64, 1024), F32)],
        grant=6,
        nbytes=3 * MIB,
    )
    return attn_out[None], jnp.transpose(grad_w, (1, 0, 2))


def solution(mesh):
    grid = Mesh(mesh.devices.reshape(4, 4, 2, 8), ("y", "x", "core", "dp"))
    seq = ("y", "x", "core")
    return jax.shard_map(
        per_device,
        mesh=grid,
        in_specs=(P("dp", seq, None), P(seq, None, None), P(), P("dp", seq, None), P("dp", seq, None)),
        out_specs=(P("dp", seq, None), P(seq, None, None)),
        check_vma=False,
    )
```

profile of v0, /device:TPU:6, one launch (start us, length us, event | category | flops | bytes accessed | tf_op | source)
XLA Modules:
  0.0 164.5 jit_solution(5728479668793557477)
XLA Ops:
  5.3 2.8 %collective-permute-start.5 = (bf16[128,768]{1,0:T(8,128)(2,1)S(1)}, bf16[128,768]{1,0:T(8,128)(2,1)S(1)}, u32[]{:S(2)}, u32[]{:S(2)}) collective-permute-start(bf16[128,768]{1,0:T(8,128)(2,1)S(1)} %get-tuple-element.62), channel_id=1, source_target_pairs={{0,32},{8,136},{16,48},{24,152},{32,0},{40,168},{48,16},{56,184},{... | collective-permute-start | bytes 589832 | tf_op jit(solution)/shard_map/ppermute | solution.py:29
  8.3 2.1 %collective-permute-start.6 = (bf16[128,768]{1,0:T(8,128)(2,1)S(1)}, bf16[128,768]{1,0:T(8,128)(2,1)S(1)}, u32[]{:S(2)}, u32[]{:S(2)}) collective-permute-start(bf16[128,768]{1,0:T(8,128)(2,1)S(1)} %get-tuple-element.62), channel_id=1, source_target_pairs={{0,16},{8,72},{16,32},{24,88},{32,48},{40,104},{48,0},{56,120},{64... | collective-permute-start | bytes 589832 | tf_op jit(solution)/shard_map/ppermute | solution.py:29
  12.0 1.9 %collective-permute-done.5 = bf16[128,768]{1,0:T(8,128)(2,1)S(1)} collective-permute-done((bf16[128,768]{1,0:T(8,128)(2,1)S(1)}, bf16[128,768]{1,0:T(8,128)(2,1)S(1)}, u32[]{:S(2)}, u32[]{:S(2)}) %collective-permute-start.5) | collective-permute-done | bytes 196640 | tf_op jit(solution)/shard_map/ppermute | solution.py:29
  15.3 1.8 %collective-permute-start.8 = (bf16[512,768]{1,0:T(8,128)(2,1)}, bf16[512,768]{1,0:T(8,128)(2,1)}, u32[]{:S(2)}, u32[]{:S(2)}) collective-permute-start(bf16[512,768]{1,0:T(8,128)(2,1)} %constant_dynamic-update-slice_fusion.2.refs_7_), channel_id=1, source_target_pairs={{0,64},{8,24},{16,80},{24,40},{32,96},{40,56},{48,112},{56,8},{64,... | collective-permute-start | bytes 2359304 | tf_op jit(solution)/shard_map/ppermute | solution.py:29
  18.6 14.6 %collective-permute-done.2.refs_1_.t1 = bf16[256,2048]{1,0:T(8,128)(2,1)S(1)} collective-permute-done((bf16[256,2048]{1,0:T(8,128)(2,1)}, bf16[256,2048]{1,0:T(8,128)(2,1)S(1)}, u32[]{:S(2)}, u32[]{:S(2)}) %collective-permute-start.2) | collective-permute-done | bytes 1048608 | tf_op jit(solution)/shard_map/ppermute | solution.py:33
  36.6 1.8 %slice.77 = bf16[256,768]{1,0:T(8,128)(2,1)} slice(bf16[512,768]{1,0:T(8,128)(2,1)} %collective-permute-done.12.refs_8_), slice={[256:512], [0:768]} | slice | bytes 786432 | tf_op jit(solution)/shard_map/slice | solution.py:323
  39.5 1.8 %slice.76 = bf16[256,768]{1,0:T(8,128)(2,1)} slice(bf16[512,768]{1,0:T(8,128)(2,1)} %collective-permute-done.8.refs_9_), slice={[0:256], [0:768]} | slice | bytes 786432 | tf_op jit(solution)/shard_map/slice | solution.py:323
  41.2 2.3 %collective-permute-done = s32[1,12]{1,0:T(1,128)S(1)} collective-permute-done((s32[1,12]{1,0:T(1,128)S(1)}, s32[1,12]{1,0:T(1,128)S(1)}, u32[]{:S(2)}, u32[]{:S(2)}) %collective-permute-start) | collective-permute-done | bytes 80 | tf_op jit(solution)/shard_map/ppermute | solution.py:33
  48.3 4.5 %collective-permute-done.13.refs_10_ = bf16[256,768]{1,0:T(8,128)(2,1)} collective-permute-done((bf16[256,768]{1,0:T(8,128)(2,1)}, bf16[256,768]{1,0:T(8,128)(2,1)}, u32[]{:S(2)}, u32[]{:S(2)}) %collective-permute-start.13) | collective-permute-done | bytes 393248 | tf_op jit(solution)/shard_map/ppermute | solution.py:29
  52.8 9.5 %shard_map.70 = (bf16[4,256,768]{2,1,0:T(8,128)(2,1)}, bf16[4,256,256]{2,1,0:T(8,128)(2,1)S(1)}, bf16[4,2,128,128]{3,2,1,0:T(8,128)(2,1)S(1)}, bf16[2,2,128,128]...) custom-call(s32[7]{0:T(128)S(1)} %stack.55.pos, ...), custom_call_target="tpu_custom_call" | custom-call | flops 3221225472 | bytes 10485760 | tf_op jit(solution)/shard_map/pallas_call | solution.py:61
  62.4 2.2 %collective-permute-start.23 = (bf16[2,2,128,128]{3,2,1,0:T(8,128)(2,1)S(1)}, bf16[2,2,128,128]{3,2,1,0:T(8,128)(2,1)S(1)}, u32[]{:S(2)}, u32[]{:S(2)}) collective-permute-start(bf16[2,2,128,128]{3,2,1,0:T(8,128)(2,1)S(1)} %get-tuple-element.42), channel_id=1, source_target_pairs={{0,192},{64,128},{128,64},{192,0},{1,193},{65,129},{129,65},{193,1... | collective-permute-start | bytes 393224 | tf_op jit(solution)/shard_map/ppermute | solution.py:33
  64.5 1.9 %collective-permute-start.22 = (bf16[2,2,128,128]{3,2,1,0:T(8,128)(2,1)S(1)}, bf16[2,2,128,128]{3,2,1,0:T(8,128)(2,1)S(1)}, u32[]{:S(2)}, u32[]{:S(2)}) collective-permute-start(bf16[2,2,128,128]{3,2,1,0:T(8,128)(2,1)S(1)} %get-tuple-element.42), channel_id=1, source_target_pairs={{0,128},{64,192},{128,0},{192,64},{1,129},{65,193},{129,1},{193,65... | collective-permute-start | bytes 393224 | tf_op jit(solution)/shard_map/ppermute | solution.py:33
  66.9 2.4 %collective-permute-start.16 = (bf16[2,2,128,128]{3,2,1,0:T(8,128)(2,1)S(1)}, bf16[2,2,128,128]{3,2,1,0:T(8,128)(2,1)S(1)}, u32[]{:S(2)}, u32[]{:S(2)}) collective-permute-start(bf16[2,2,128,128]{3,2,1,0:T(8,128)(2,1)S(1)} %get-tuple-element.40), channel_id=1, source_target_pairs={{0,32},{16,48},{32,0},{48,16},{1,33},{17,49},{33,1},{49,17},{2,34}... | collective-permute-start | bytes 393224 | tf_op jit(solution)/shard_map/ppermute | solution.py:33
  72.1 2.2 %collective-permute-start.25 = (bf16[2,2,128,128]{3,2,1,0:T(8,128)(2,1)S(1)}, bf16[2,2,128,128]{3,2,1,0:T(8,128)(2,1)S(1)}, u32[]{:S(2)}, u32[]{:S(2)}) collective-permute-start(bf16[2,2,128,128]{3,2,1,0:T(8,128)(2,1)S(1)} %get-tuple-element.57), channel_id=1, source_target_pairs={{0,32},{16,48},{32,0},{48,16},{1,33},{17,49},{33,1},{49,17},{2,34}... | collective-permute-start | bytes 393224 | tf_op jit(solution)/shard_map/ppermute | solution.py:33
  78.7 1.9 %collective-permute-done.24.refs_16_ = bf16[2,2,128,128]{3,2,1,0:T(8,128)(2,1)S(1)} collective-permute-done((bf16[2,2,128,128]{3,2,1,0:T(8,128)(2,1)S(1)}, bf16[2,2,128,128]{3,2,1,0:T(8,128)(2,1)S(1)}, u32[]{:S(2)}, u32[]{:S(2)}) %collective-permute-start.24) | collective-permute-done | bytes 131104 | tf_op jit(solution)/shard_map/ppermute | solution.py:33
  81.2 5.1 %shard_map.71.refs_6_ = f32[4,256,1024]{2,1,0:T(8,128)S(1)} custom-call(s32[7]{0:T(128)S(1)} %stack.55.pos, s32[4,12]{1,0:T(4,128)S(1)} %pad_add_fusion.idx, f32[16,8]{1,0:T(8,128)S(1)} %copy.9.table, bf16[4,256,768]{2,1,0:T(8,128)(2,1)S(1)} %copy-done, bf16[4,256,256]{2,1,0:T(8,128)(2,1)S(1)} %get-tuple-element.36.cots.refs_4_), custom_call_target="tpu_custom_call" | custom-call | flops 805306368 | bytes 8388608 | tf_op jit(solution)/shard_map/pallas_call | solution.py:61
  86.4 3.9 %shard_map.72 = (bf16[4,256,256]{2,1,0:T(8,128)(2,1)S(1)}, bf16[4,256,768]{2,1,0:T(8,128)(2,1)S(1)}, bf16[2,128,768]{2,1,0:T(8,128)(2,1)S(1)}, bf16[2,128,768]{2,1,0:T(8,128)(2,1)S(1)}) custom-call(s32[7]{0:T(128)S(1)} %stack.55.pos, s32[4,12]{1,0:T(4,128)S(1)} %pad_add_fusion.idx, f32[16,8]{1,0:T(8,128)S(1)} %copy.9.table, bf16[256,2048]{1,0:T(8,128)(2,1)S(1)} %bitcast.31, ...), custom_call_target="tpu_custom_call" | custom-call | flops 1610612736 | bytes 12582912 | tf_op jit(solution)/shard_map/pallas_call | solution.py:61
  92.4 4.2 %shard_map.73 = (bf16[4,128,768]{2,1,0:T(8,128)(2,1)S(1)}, bf16[4,128,768]{2,1,0:T(8,128)(2,1)S(1)}, bf16[4,128,768]{2,1,0:T(8,128)(2,1)S(1)}) custom-call(s32[7]{0:T(128)S(1)} %stack.55.pos, bf16[256,2048]{1,0:T(8,128)(2,1)S(1)} %bitcast.32, bf16[256,2048]{1,0:T(8,128)(2,1)S(1)} %copy-done.4, bf16[256,2048]{1,0:T(8,128)(2,1)S(1)} %copy-done.6, ...), custom_call_target="tpu_custom_call" | custom-call | flops 3221225472 | bytes 9437184 | tf_op jit(solution)/shard_map/pallas_call | solution.py:61
  98.3 2.9 %collective-permute-start.32 = (bf16[4,128,768]{2,1,0:T(8,128)(2,1)S(1)}, bf16[4,128,768]{2,1,0:T(8,128)(2,1)S(1)}, u32[]{:S(2)}, u32[]{:S(2)}) collective-permute-start(bf16[4,128,768]{2,1,0:T(8,128)(2,1)S(1)} %pad_maximum_fusion.1), channel_id=1, source_target_pairs={{0,192},{8,56},{16,208},{24,8},{32,224},{40,24},{48,240},{56,40},{... | collective-permute-start | bytes 2359304 | tf_op jit(solution)/shard_map/ppermute | solution.py:29
  101.7 9.0 %collective-permute-done.32 = bf16[4,128,768]{2,1,0:T(8,128)(2,1)S(1)} collective-permute-done((bf16[4,128,768]{2,1,0:T(8,128)(2,1)S(1)}, bf16[4,128,768]{2,1,0:T(8,128)(2,1)S(1)}, u32[]{:S(2)}, u32[]{:S(2)}) %collective-permute-start.32) | collective-permute-done | bytes 786464 | tf_op jit(solution)/shard_map/ppermute | solution.py:29
  110.7 8.4 %collective-permute-done.30 = bf16[4,128,768]{2,1,0:T(8,128)(2,1)S(1)} collective-permute-done((bf16[4,128,768]{2,1,0:T(8,128)(2,1)S(1)}, bf16[4,128,768]{2,1,0:T(8,128)(2,1)S(1)}, u32[]{:S(2)}, u32[]{:S(2)}) %collective-permute-start.30) | collective-permute-done | bytes 786464 | tf_op jit(solution)/shard_map/ppermute | solution.py:29
  119.4 2.6 %collective-permute-start.33 = (bf16[128,768]{1,0:T(8,128)(2,1)S(1)}, bf16[128,768]{1,0:T(8,128)(2,1)S(1)}, u32[]{:S(2)}, u32[]{:S(2)}) collective-permute-start(bf16[128,768]{1,0:T(8,128)(2,1)S(1)} %get-tuple-element.54), channel_id=1, source_target_pairs={{0,16},{8,72},{16,32},{24,88},{32,48},{40,104},{48,0},{56,120},{64... | collective-permute-start | bytes 589832 | tf_op jit(solution)/shard_map/ppermute | solution.py:29
  122.0 1.9 %collective-permute-start.34 = (bf16[128,768]{1,0:T(8,128)(2,1)S(1)}, bf16[128,768]{1,0:T(8,128)(2,1)S(1)}, u32[]{:S(2)}, u32[]{:S(2)}) collective-permute-start(bf16[128,768]{1,0:T(8,128)(2,1)S(1)} %get-tuple-element.56), channel_id=1, source_target_pairs={{0,32},{8,136},{16,48},{24,152},{32,0},{40,168},{48,16},{56,184},{... | collective-permute-start | bytes 589832 | tf_op jit(solution)/shard_map/ppermute | solution.py:29
  125.2 5.8 %collective-permute-done.35 = bf16[128,768]{1,0:T(8,128)(2,1)S(1)} collective-permute-done((bf16[128,768]{1,0:T(8,128)(2,1)S(1)}, bf16[128,768]{1,0:T(8,128)(2,1)S(1)}, u32[]{:S(2)}, u32[]{:S(2)}) %collective-permute-start.35) | collective-permute-done | bytes 196640 | tf_op jit(solution)/shard_map/ppermute | solution.py:29
  132.5 5.3 %collective-permute-start.37 = (bf16[2,32,768]{2,1,0:T(8,128)(2,1)S(1)}, bf16[2,32,768]{2,1,0:T(8,128)(2,1)S(1)}, u32[]{:S(2)}, u32[]{:S(2)}) collective-permute-start(bf16[2,32,768]{2,1,0:T(8,128)(2,1)S(1)} %pad_maximum_fusion.5), channel_id=1, source_target_pairs={{0,7},{1,2},{2,1},{3,4},{4,3},{5,6},{6,5},{7,0},{8,15},{9,10},{10,... | collective-permute-start | bytes 294920 | tf_op jit(solution)/shard_map/ppermute | solution.py:37
  138.0 2.9 %collective-permute-done.37 = bf16[2,32,768]{2,1,0:T(8,128)(2,1)S(1)} collective-permute-done((bf16[2,32,768]{2,1,0:T(8,128)(2,1)S(1)}, bf16[2,32,768]{2,1,0:T(8,128)(2,1)S(1)}, u32[]{:S(2)}, u32[]{:S(2)}) %collective-permute-start.37) | collective-permute-done | bytes 98336 | tf_op jit(solution)/shard_map/ppermute | solution.py:37
  140.9 2.0 %collective-permute-start.38 = (bf16[2,32,768]{2,1,0:T(8,128)(2,1)S(1)}, bf16[2,32,768]{2,1,0:T(8,128)(2,1)S(1)}, u32[]{:S(2)}, u32[]{:S(2)}) collective-permute-start(bf16[2,32,768]{2,1,0:T(8,128)(2,1)S(1)} %add_convert_fusion.7), channel_id=1, source_target_pairs={{0,3},{1,6},{2,5},{3,0},{4,7},{5,2},{6,1},{7,4},{8,11},{9,14},{10,... | collective-permute-start | bytes 294920 | tf_op jit(solution)/shard_map/ppermute | solution.py:41
  143.0 6.4 %collective-permute-done.38 = bf16[2,32,768]{2,1,0:T(8,128)(2,1)S(1)} collective-permute-done((bf16[2,32,768]{2,1,0:T(8,128)(2,1)S(1)}, bf16[2,32,768]{2,1,0:T(8,128)(2,1)S(1)}, u32[]{:S(2)}, u32[]{:S(2)}) %collective-permute-start.38) | collective-permute-done | bytes 98336 | tf_op jit(solution)/shard_map/ppermute | solution.py:41
  149.4 2.7 %collective-permute-start.39 = (bf16[2,32,768]{2,1,0:T(8,128)(2,1)S(1)}, bf16[2,32,768]{2,1,0:T(8,128)(2,1)S(1)}, u32[]{:S(2)}, u32[]{:S(2)}) collective-permute-start(bf16[2,32,768]{2,1,0:T(8,128)(2,1)S(1)} %add_convert_fusion.6.mine), channel_id=1, source_target_pairs={{0,7},{1,2},{2,1},{3,4},{4,3},{5,6},{6,5},{7,0},{8,15},{9,10},{10,... | collective-permute-start | bytes 294920 | tf_op jit(solution)/shard_map/ppermute | solution.py:37
  152.2 3.1 %collective-permute-done.39.near = bf16[2,32,768]{2,1,0:T(8,128)(2,1)S(1)} collective-permute-done((bf16[2,32,768]{2,1,0:T(8,128)(2,1)S(1)}, bf16[2,32,768]{2,1,0:T(8,128)(2,1)S(1)}, u32[]{:S(2)}, u32[]{:S(2)}) %collective-permute-start.39) | collective-permute-done | bytes 98336 | tf_op jit(solution)/shard_map/ppermute | solution.py:37
  155.4 5.3 %collective-permute-done.28.from_z = bf16[2,256,256]{2,1,0:T(8,128)(2,1)S(1)} collective-permute-done((bf16[2,256,256]{2,1,0:T(8,128)(2,1)S(1)}, bf16[2,256,256]{2,1,0:T(8,128)(2,1)S(1)}, u32[]{:S(2)}, u32[]{:S(2)}) %collective-permute-start.28) | collective-permute-done | bytes 262176 | tf_op jit(solution)/shard_map/ppermute | solution.py:33
  160.7 2.1 %collective-permute-done.40.theirs = bf16[2,2,32,768]{3,2,1,0:T(8,128)(2,1)S(1)} collective-permute-done((bf16[2,2,32,768]{3,2,1,0:T(8,128)(2,1)S(1)}, bf16[2,2,32,768]{3,2,1,0:T(8,128)(2,1)S(1)}, u32[]{:S(2)}, u32[]{:S(2)}) %collective-permute-start.40) | collective-permute-done | bytes 196640 | tf_op jit(solution)/shard_map/ppermute | solution.py:33
  (114 shorter events, 36.2 us)
Async XLA Ops:
  4.5 6.9 %collective-permute-start.4 = (bf16[128,768]{1,0:T(8,128)(2,1)S(1)}, bf16[128,768]{1,0:T(8,128)(2,1)S(1)}, u32[]{:S(2)}, u32[]{:S(2)}) collective-permute-start(bf16[128,768]{1,0:T(8,128)(2,1)S(1)} %get-tuple-element.62), channel_id=1, source_target_pairs={{0,48},{8,200},{16,0},{24,216},{32,16},{40,232},{48,32},{56,248},{... | collective-permute-start | bytes 589832 | tf_op jit(solution)/shard_map/ppermute | solution.py:29
  5.3 8.6 %collective-permute-start.5 = (bf16[128,768]{1,0:T(8,128)(2,1)S(1)}, bf16[128,768]{1,0:T(8,128)(2,1)S(1)}, u32[]{:S(2)}, u32[]{:S(2)}) collective-permute-start(bf16[128,768]{1,0:T(8,128)(2,1)S(1)} %get-tuple-element.62), channel_id=1, source_target_pairs={{0,32},{8,136},{16,48},{24,152},{32,0},{40,168},{48,16},{56,184},{... | collective-permute-start | bytes 589832 | tf_op jit(solution)/shard_map/ppermute | solution.py:29
  8.1 25.0 %collective-permute-start.2 = (bf16[256,2048]{1,0:T(8,128)(2,1)}, bf16[256,2048]{1,0:T(8,128)(2,1)S(1)}, u32[]{:S(2)}, u32[]{:S(2)}) collective-permute-start(bf16[256,2048]{1,0:T(8,128)(2,1)} %bitcast.28), channel_id=1, source_target_pairs={{0,1},{1,0},{2,3},{3,2},{4,5},{5,4},{6,7},{7,6},{8,9},{9,8},{10,11... | collective-permute-start | bytes 3145736 | tf_op jit(solution)/shard_map/ppermute | solution.py:33
  8.3 6.3 %collective-permute-start.6 = (bf16[128,768]{1,0:T(8,128)(2,1)S(1)}, bf16[128,768]{1,0:T(8,128)(2,1)S(1)}, u32[]{:S(2)}, u32[]{:S(2)}) collective-permute-start(bf16[128,768]{1,0:T(8,128)(2,1)S(1)} %get-tuple-element.62), channel_id=1, source_target_pairs={{0,16},{8,72},{16,32},{24,88},{32,48},{40,104},{48,0},{56,120},{64... | collective-permute-start | bytes 589832 | tf_op jit(solution)/shard_map/ppermute | solution.py:29
  15.3 17.9 %collective-permute-start.8 = (bf16[512,768]{1,0:T(8,128)(2,1)}, bf16[512,768]{1,0:T(8,128)(2,1)}, u32[]{:S(2)}, u32[]{:S(2)}) collective-permute-start(bf16[512,768]{1,0:T(8,128)(2,1)} %constant_dynamic-update-slice_fusion.2.refs_7_), channel_id=1, source_target_pairs={{0,64},{8,24},{16,80},{24,40},{32,96},{40,56},{48,112},{56,8},{64,... | collective-permute-start | bytes 2359304 | tf_op jit(solution)/shard_map/ppermute | solution.py:29
  17.1 19.5 %collective-permute-start.12 = (bf16[512,768]{1,0:T(8,128)(2,1)}, bf16[512,768]{1,0:T(8,128)(2,1)}, u32[]{:S(2)}, u32[]{:S(2)}) collective-permute-start(bf16[512,768]{1,0:T(8,128)(2,1)} %constant_dynamic-update-slice_fusion.2.refs_7_), channel_id=1, source_target_pairs={{0,192},{8,56},{16,208},{24,8},{32,224},{40,24},{48,240},{56,40},{... | collective-permute-start | bytes 2359304 | tf_op jit(solution)/shard_map/ppermute | solution.py:29
  18.6 29.8 %collective-permute-start.7 = (bf16[256,2048]{1,0:T(8,128)(2,1)S(1)}, bf16[256,2048]{1,0:T(8,128)(2,1)S(1)}, u32[]{:S(2)}, u32[]{:S(2)}) collective-permute-start(bf16[256,2048]{1,0:T(8,128)(2,1)S(1)} %bitcast.30), channel_id=1, source_target_pairs={{0,8},{8,0},{1,9},{9,1},{2,10},{10,2},{3,11},{11,3},{4,12},{12,4},... | collective-permute-start | bytes 3145736 | tf_op jit(solution)/shard_map/ppermute | solution.py:33
  33.2 19.7 %collective-permute-start.9 = (bf16[256,2048]{1,0:T(8,128)(2,1)S(1)}, bf16[256,2048]{1,0:T(8,128)(2,1)}, u32[]{:S(2)}, u32[]{:S(2)}) collective-permute-start(bf16[256,2048]{1,0:T(8,128)(2,1)S(1)} %collective-permute-done.2.refs_1_.t1), channel_id=1, source_target_pairs={{0,8},{8,0},{1,9},{9,1},{2,10},{10,2},{3,11},{11,3},{4,12},{12,4},... | collective-permute-start | bytes 3145736 | tf_op jit(solution)/shard_map/ppermute | solution.py:33
  34.5 10.0 %collective-permute-start.10 = (bf16[2,256,256]{2,1,0:T(8,128)(2,1)}, bf16[2,256,256]{2,1,0:T(8,128)(2,1)}, u32[]{:S(2)}, u32[]{:S(2)}) collective-permute-start(bf16[2,256,256]{2,1,0:T(8,128)(2,1)} %get-tuple-element.34), channel_id=1, source_target_pairs={{0,1},{1,0},{2,3},{3,2},{4,5},{5,4},{6,7},{7,6},{8,9},{9,8},{10,11... | collective-permute-start | bytes 786440 | tf_op jit(solution)/shard_map/ppermute | solution.py:33
  35.8 7.7 %collective-permute-start = (s32[1,12]{1,0:T(1,128)S(1)}, s32[1,12]{1,0:T(1,128)S(1)}, u32[]{:S(2)}, u32[]{:S(2)}) collective-permute-start(s32[1,12]{1,0:T(1,128)S(1)} %reshape.9), channel_id=1, source_target_pairs={{0,1},{1,0},{2,3},{3,2},{4,5},{5,4},{6,7},{7,6},{8,9},{9,8},{10,11... | collective-permute-start | bytes 152 | tf_op jit(solution)/shard_map/ppermute | solution.py:33
  38.4 9.9 %collective-permute-start.14 = (bf16[256,768]{1,0:T(8,128)(2,1)}, bf16[256,768]{1,0:T(8,128)(2,1)}, u32[]{:S(2)}, u32[]{:S(2)}) collective-permute-start(bf16[256,768]{1,0:T(8,128)(2,1)} %slice.77), channel_id=1, source_target_pairs={{0,192},{8,56},{16,208},{24,8},{32,224},{40,24},{48,240},{56,40},{... | collective-permute-start | bytes 1179656 | tf_op jit(solution)/shard_map/ppermute | solution.py:29
  43.5 9.3 %collective-permute-start.13 = (bf16[256,768]{1,0:T(8,128)(2,1)}, bf16[256,768]{1,0:T(8,128)(2,1)}, u32[]{:S(2)}, u32[]{:S(2)}) collective-permute-start(bf16[256,768]{1,0:T(8,128)(2,1)} %slice.76), channel_id=1, source_target_pairs={{0,64},{8,24},{16,80},{24,40},{32,96},{40,56},{48,112},{56,8},{64,... | collective-permute-start | bytes 1179656 | tf_op jit(solution)/shard_map/ppermute | solution.py:29
  62.4 7.0 %collective-permute-start.21 = (bf16[2,2,128,128]{3,2,1,0:T(8,128)(2,1)S(1)}, bf16[2,2,128,128]{3,2,1,0:T(8,128)(2,1)S(1)}, u32[]{:S(2)}, u32[]{:S(2)}) collective-permute-start(bf16[2,2,128,128]{3,2,1,0:T(8,128)(2,1)S(1)} %get-tuple-element.41), channel_id=1, source_target_pairs={{0,64},{64,0},{128,192},{192,128},{1,65},{65,1},{129,193},{193,129... | collective-permute-start | bytes 393224 | tf_op jit(solution)/shard_map/ppermute | solution.py:33
  62.4 8.9 %collective-permute-start.23 = (bf16[2,2,128,128]{3,2,1,0:T(8,128)(2,1)S(1)}, bf16[2,2,128,128]{3,2,1,0:T(8,128)(2,1)S(1)}, u32[]{:S(2)}, u32[]{:S(2)}) collective-permute-start(bf16[2,2,128,128]{3,2,1,0:T(8,128)(2,1)S(1)} %get-tuple-element.42), channel_id=1, source_target_pairs={{0,192},{64,128},{128,64},{192,0},{1,193},{65,129},{129,65},{193,1... | collective-permute-start | bytes 393224 | tf_op jit(solution)/shard_map/ppermute | solution.py:33
  64.5 6.7 %collective-permute-start.22 = (bf16[2,2,128,128]{3,2,1,0:T(8,128)(2,1)S(1)}, bf16[2,2,128,128]{3,2,1,0:T(8,128)(2,1)S(1)}, u32[]{:S(2)}, u32[]{:S(2)}) collective-permute-start(bf16[2,2,128,128]{3,2,1,0:T(8,128)(2,1)S(1)} %get-tuple-element.42), channel_id=1, source_target_pairs={{0,128},{64,192},{128,0},{192,64},{1,129},{65,193},{129,1},{193,65... | collective-permute-start | bytes 393224 | tf_op jit(solution)/shard_map/ppermute | solution.py:33
  66.5 8.2 %collective-permute-start.17 = (bf16[2,2,128,128]{3,2,1,0:T(8,128)(2,1)S(1)}, bf16[2,2,128,128]{3,2,1,0:T(8,128)(2,1)S(1)}, u32[]{:S(2)}, u32[]{:S(2)}) collective-permute-start(bf16[2,2,128,128]{3,2,1,0:T(8,128)(2,1)S(1)} %get-tuple-element.40), channel_id=1, source_target_pairs={{0,48},{16,32},{32,16},{48,0},{1,49},{17,33},{33,17},{49,1},{2,50}... | collective-permute-start | bytes 393224 | tf_op jit(solution)/shard_map/ppermute | solution.py:33
  66.9 8.6 %collective-permute-start.16 = (bf16[2,2,128,128]{3,2,1,0:T(8,128)(2,1)S(1)}, bf16[2,2,128,128]{3,2,1,0:T(8,128)(2,1)S(1)}, u32[]{:S(2)}, u32[]{:S(2)}) collective-permute-start(bf16[2,2,128,128]{3,2,1,0:T(8,128)(2,1)S(1)} %get-tuple-element.40), channel_id=1, source_target_pairs={{0,32},{16,48},{32,0},{48,16},{1,33},{17,49},{33,1},{49,17},{2,34}... | collective-permute-start | bytes 393224 | tf_op jit(solution)/shard_map/ppermute | solution.py:33
  69.4 7.6 %collective-permute-start.15 = (bf16[2,2,128,128]{3,2,1,0:T(8,128)(2,1)S(1)}, bf16[2,2,128,128]{3,2,1,0:T(8,128)(2,1)S(1)}, u32[]{:S(2)}, u32[]{:S(2)}) collective-permute-start(bf16[2,2,128,128]{3,2,1,0:T(8,128)(2,1)S(1)} %get-tuple-element.40), channel_id=1, source_target_pairs={{0,16},{16,0},{32,48},{48,32},{1,17},{17,1},{33,49},{49,33},{2,18}... | collective-permute-start | bytes 393224 | tf_op jit(solution)/shard_map/ppermute | solution.py:33
  71.4 14.9 %collective-permute-start.26 = (bf16[2,2,128,128]{3,2,1,0:T(8,128)(2,1)S(1)}, bf16[2,2,128,128]{3,2,1,0:T(8,128)(2,1)S(1)}, u32[]{:S(2)}, u32[]{:S(2)}) collective-permute-start(bf16[2,2,128,128]{3,2,1,0:T(8,128)(2,1)S(1)} %get-tuple-element.57), channel_id=1, source_target_pairs={{0,48},{16,32},{32,16},{48,0},{1,49},{17,33},{33,17},{49,1},{2,50}... | collective-permute-start | bytes 393224 | tf_op jit(solution)/shard_map/ppermute | solution.py:33
  72.1 14.2 %collective-permute-start.25 = (bf16[2,2,128,128]{3,2,1,0:T(8,128)(2,1)S(1)}, bf16[2,2,128,128]{3,2,1,0:T(8,128)(2,1)S(1)}, u32[]{:S(2)}, u32[]{:S(2)}) collective-permute-start(bf16[2,2,128,128]{3,2,1,0:T(8,128)(2,1)S(1)} %get-tuple-element.57), channel_id=1, source_target_pairs={{0,32},{16,48},{32,0},{48,16},{1,33},{17,49},{33,1},{49,17},{2,34}... | collective-permute-start | bytes 393224 | tf_op jit(solution)/shard_map/ppermute | solution.py:33
  77.0 9.3 %collective-permute-start.20 = (bf16[2,2,128,128]{3,2,1,0:T(8,128)(2,1)S(1)}, bf16[2,2,128,128]{3,2,1,0:T(8,128)(2,1)S(1)}, u32[]{:S(2)}, u32[]{:S(2)}) collective-permute-start(bf16[2,2,128,128]{3,2,1,0:T(8,128)(2,1)S(1)} %add_convert_fusion.5), channel_id=1, source_target_pairs={{0,192},{64,128},{128,64},{192,0},{1,193},{65,129},{129,65},{193,1... | collective-permute-start | bytes 393224 | tf_op jit(solution)/shard_map/ppermute | solution.py:33
  77.1 9.2 %collective-permute-start.19 = (bf16[2,2,128,128]{3,2,1,0:T(8,128)(2,1)S(1)}, bf16[2,2,128,128]{3,2,1,0:T(8,128)(2,1)S(1)}, u32[]{:S(2)}, u32[]{:S(2)}) collective-permute-start(bf16[2,2,128,128]{3,2,1,0:T(8,128)(2,1)S(1)} %add_convert_fusion.5), channel_id=1, source_target_pairs={{0,128},{64,192},{128,0},{192,64},{1,129},{65,193},{129,1},{193,65... | collective-permute-start | bytes 393224 | tf_op jit(solution)/shard_map/ppermute | solution.py:33
  90.3 7.9 %collective-permute-start.31 = (bf16[2,128,768]{2,1,0:T(8,128)(2,1)S(1)}, bf16[2,128,768]{2,1,0:T(8,128)(2,1)S(1)}, u32[]{:S(2)}, u32[]{:S(2)}) collective-permute-start(bf16[2,128,768]{2,1,0:T(8,128)(2,1)S(1)} %get-tuple-element.51), channel_id=1, source_target_pairs={{0,192},{8,56},{16,208},{24,8},{32,224},{40,24},{48,240},{56,40},{... | collective-permute-start | bytes 1179656 | tf_op jit(solution)/shard_map/ppermute | solution.py:29
  91.9 9.2 %collective-permute-start.29 = (bf16[2,128,768]{2,1,0:T(8,128)(2,1)S(1)}, bf16[2,128,768]{2,1,0:T(8,128)(2,1)S(1)}, u32[]{:S(2)}, u32[]{:S(2)}) collective-permute-start(bf16[2,128,768]{2,1,0:T(8,128)(2,1)S(1)} %get-tuple-element.49), channel_id=1, source_target_pairs={{0,64},{8,24},{16,80},{24,40},{32,96},{40,56},{48,112},{56,8},{64,... | collective-permute-start | bytes 1179656 | tf_op jit(solution)/shard_map/ppermute | solution.py:29
  98.3 12.4 %collective-permute-start.32 = (bf16[4,128,768]{2,1,0:T(8,128)(2,1)S(1)}, bf16[4,128,768]{2,1,0:T(8,128)(2,1)S(1)}, u32[]{:S(2)}, u32[]{:S(2)}) collective-permute-start(bf16[4,128,768]{2,1,0:T(8,128)(2,1)S(1)} %pad_maximum_fusion.1), channel_id=1, source_target_pairs={{0,192},{8,56},{16,208},{24,8},{32,224},{40,24},{48,240},{56,40},{... | collective-permute-start | bytes 2359304 | tf_op jit(solution)/shard_map/ppermute | solution.py:29
  101.3 17.7 %collective-permute-start.30 = (bf16[4,128,768]{2,1,0:T(8,128)(2,1)S(1)}, bf16[4,128,768]{2,1,0:T(8,128)(2,1)S(1)}, u32[]{:S(2)}, u32[]{:S(2)}) collective-permute-start(bf16[4,128,768]{2,1,0:T(8,128)(2,1)S(1)} %pad_maximum_fusion), channel_id=1, source_target_pairs={{0,64},{8,24},{16,80},{24,40},{32,96},{40,56},{48,112},{56,8},{64,... | collective-permute-start | bytes 2359304 | tf_op jit(solution)/shard_map/ppermute | solution.py:29
  122.0 9.0 %collective-permute-start.35 = (bf16[128,768]{1,0:T(8,128)(2,1)S(1)}, bf16[128,768]{1,0:T(8,128)(2,1)S(1)}, u32[]{:S(2)}, u32[]{:S(2)}) collective-permute-start(bf16[128,768]{1,0:T(8,128)(2,1)S(1)} %get-tuple-element.55), channel_id=1, source_target_pairs={{0,48},{8,200},{16,0},{24,216},{32,16},{40,232},{48,32},{56,248},{... | collective-permute-start | bytes 589832 | tf_op jit(solution)/shard_map/ppermute | solution.py:29
  122.0 9.0 %collective-permute-start.34 = (bf16[128,768]{1,0:T(8,128)(2,1)S(1)}, bf16[128,768]{1,0:T(8,128)(2,1)S(1)}, u32[]{:S(2)}, u32[]{:S(2)}) collective-permute-start(bf16[128,768]{1,0:T(8,128)(2,1)S(1)} %get-tuple-element.56), channel_id=1, source_target_pairs={{0,32},{8,136},{16,48},{24,152},{32,0},{40,168},{48,16},{56,184},{... | collective-permute-start | bytes 589832 | tf_op jit(solution)/shard_map/ppermute | solution.py:29
  132.5 8.4 %collective-permute-start.37 = (bf16[2,32,768]{2,1,0:T(8,128)(2,1)S(1)}, bf16[2,32,768]{2,1,0:T(8,128)(2,1)S(1)}, u32[]{:S(2)}, u32[]{:S(2)}) collective-permute-start(bf16[2,32,768]{2,1,0:T(8,128)(2,1)S(1)} %pad_maximum_fusion.5), channel_id=1, source_target_pairs={{0,7},{1,2},{2,1},{3,4},{4,3},{5,6},{6,5},{7,0},{8,15},{9,10},{10,... | collective-permute-start | bytes 294920 | tf_op jit(solution)/shard_map/ppermute | solution.py:37
  140.9 8.4 %collective-permute-start.38 = (bf16[2,32,768]{2,1,0:T(8,128)(2,1)S(1)}, bf16[2,32,768]{2,1,0:T(8,128)(2,1)S(1)}, u32[]{:S(2)}, u32[]{:S(2)}) collective-permute-start(bf16[2,32,768]{2,1,0:T(8,128)(2,1)S(1)} %add_convert_fusion.7), channel_id=1, source_target_pairs={{0,3},{1,6},{2,5},{3,0},{4,7},{5,2},{6,1},{7,4},{8,11},{9,14},{10,... | collective-permute-start | bytes 294920 | tf_op jit(solution)/shard_map/ppermute | solution.py:41
  152.1 8.6 %collective-permute-start.28 = (bf16[2,256,256]{2,1,0:T(8,128)(2,1)S(1)}, bf16[2,256,256]{2,1,0:T(8,128)(2,1)S(1)}, u32[]{:S(2)}, u32[]{:S(2)}) collective-permute-start(bf16[2,256,256]{2,1,0:T(8,128)(2,1)S(1)} %pad_maximum_fusion.3), channel_id=1, source_target_pairs={{0,1},{1,0},{2,3},{3,2},{4,5},{5,4},{6,7},{7,6},{8,9},{9,8},{10,11... | collective-permute-start | bytes 786440 | tf_op jit(solution)/shard_map/ppermute | solution.py:33
  155.3 7.5 %collective-permute-start.40 = (bf16[2,2,32,768]{3,2,1,0:T(8,128)(2,1)S(1)}, bf16[2,2,32,768]{3,2,1,0:T(8,128)(2,1)S(1)}, u32[]{:S(2)}, u32[]{:S(2)}) collective-permute-start(bf16[2,2,32,768]{3,2,1,0:T(8,128)(2,1)S(1)} %pad_maximum_fusion.4), channel_id=1, source_target_pairs={{0,1},{1,0},{2,3},{3,2},{4,5},{5,4},{6,7},{7,6},{8,9},{9,8},{10,11... | collective-permute-start | bytes 589832 | tf_op jit(solution)/shard_map/ppermute | solution.py:33
  (20 other events, 186.0 us)
where the time goes:
time: 165 us
  waiting for transfers between devices  77.6 us (47%)
  starting transfers between devices  48.4 us (29%)
  Pallas kernels  26.3 us (16%)
  local copies, waits for them, and re-layouts  9.37 us (6%)
  other arithmetic  1.78 us (1%)
    ppermute x14, waiting for transfers between devices, ring(): return lax.ppermute(value, ('y', 'x', 'core'), pairs)  33.2 us
    ppermute x24, waiting for transfers between devices, swap(): return lax.ppermute(value, axis, [(i, i ^ mask) for i in range(size)])  32 us
    pallas_call x7, Pallas kernels, call(): pl.pallas_call(kernel, out_shape=[jax.ShapeDtypeStruct(*out) for out in o...  26.3 us
    ppermute x14, starting transfers between devices, ring(): return lax.ppermute(value, ('y', 'x', 'core'), pairs)  20.9 us
    ppermute x24, starting transfers between devices, swap(): return lax.ppermute(value, axis, [(i, i ^ mask) for i in range(size)])  17.6 us
    ppermute x2, starting transfers between devices, same_set_neighbour(): lax.ppermute(value, 'dp', [(z, (z + 1 if z % 2 else z - 1) % 8) for z in...  8.03 us
    ppermute x1, waiting for transfers between devices, same_set_far(): lax.ppermute(value, 'dp', [(z, ((7 if SETS >> z & 1 else 3) - z) % 8) for...  6.37 us
    ppermute x2, waiting for transfers between devices, same_set_neighbour(): lax.ppermute(value, 'dp', [(z, (z + 1 if z % 2 else z - 1) % 8) for z in...  6 us
  transfers between devices with their start and end apart: 41, of which 22 were waited for; matrix products, arithmetic and copies ran while one was open for 5% of the time, Pallas kernels for 6%

commit v1 on v0

--- a/solution.py
+++ b/solution.py
@@ -1,3 +1,4 @@
+import functools
 import math
 
 import jax
@@ -45,6 +46,17 @@
     return lax.optimization_barrier((value, *others))[0]
 
 
+def hold(value, *others):
+    anywhere = pl.BlockSpec(memory_space=pl.ANY)
+    return pl.pallas_call(
+        lambda *refs: None,
+        out_shape=jax.ShapeDtypeStruct(value.shape, value.dtype),
+        in_specs=[anywhere] * (1 + len(others)),
+        out_specs=anywhere,
+        input_output_aliases={0: 0},
+    )(value, *others)
+
+
 def dot(a, b, ca, cb):
     return lax.dot_general(a, b, (((ca,), (cb,)), ((), ())), preferred_element_type=F32)
 
@@ -57,11 +69,13 @@
     return pl.BlockSpec(memory_space=pltpu.VMEM)
 
 
-def call(kernel, args, n_smem, outs, scratch=(), grant=16, flops=0, nbytes=0):
+def call(kernel, args, n_smem, outs, scratch=(), grant=16, flops=0, nbytes=0, n_any=0):
     return pl.pallas_call(
         kernel,
         out_shape=[jax.ShapeDtypeStruct(*out) for out in outs],
-        in_specs=[smem()] * n_smem + [vmem()] * (len(args) - n_smem),
+        in_specs=[smem()] * n_smem
+        + [vmem()] * (len(args) - n_smem - n_any)
+        + [pl.BlockSpec(memory_space=pl.ANY)] * n_any,
         out_specs=[vmem()] * len(outs),
         scratch_shapes=list(scratch),
         compiler_params=pltpu.CompilerParams(vmem_limit_bytes=grant * MIB),
@@ -84,14 +98,19 @@
     return lam * bit.astype(F32) * (1.0 / math.sqrt(HEAD * 2 ** (level - 1) * BLOCK))
 
 
-def prepare_kernel(pos, w, w_own, w_core):
+def prepare_kernel(pos, w, w_own, w_core, sems):
     core, kind = pos[2], pos[4]
-    mine = pl.multiple_of((core * 2 + kind) * 256, 256)
-    other = pl.multiple_of(((1 - core) * 2 + kind) * 256, 256)
-    for third in range(3):
-        at = slice(third * 256, third * 256 + 256)
-        w_own[:, at] = w[third, :, pl.ds(mine, 256)]
-        w_core[:, at] = w[third, :, pl.ds(other, 256)]
+    copies = []
+    for n, out in enumerate((w_core, w_own)):
+        group = ((1 - core if n == 0 else core) * 2 + kind) * 256
+        for third in range(3):
+            src = w.at[third, :, pl.ds(pl.multiple_of(group, 256), 256)]
+            dst = out.at[:, pl.ds(third * 256, 256)]
+            copies.append(pltpu.make_async_copy(src, dst, sems.at[n * 3 + third]))
+    for copy in copies:
+        copy.start()
+    for copy in copies:
+        copy.wait()
 
 
 def split_kernel(pos, cot, c_own, c_z):
@@ -103,34 +122,36 @@
 
 
 def project_kernel(pos, idx, table, *refs):
-    toks = refs[0:4]
     c_own, c_z, c_core = refs[4:7]
-    mine, ahead, behind, far_low, far_high = refs[7:12]
-    qkv, cots, s1, x0, g1, m2, m3, m4, m5, w = refs[12:]
+    parts = (refs[7:9], refs[9:11], refs[13:15], refs[11:13])
+    qkv, cots, s1, x0, g1, m2, m3, m4, m5, w, toks, sems = refs[15:]
     y, x, core = pos[0], pos[1], pos[2]
-
-    def place(part, first, slot, dist):
-        yy = (y + dist + core * (slot - dist)) & 3
-        xx = (x + slot + core * (dist - slot)) & 3
-        for cs in range(2):
-            row = pl.multiple_of((yy * 4 + xx) * 128 + ((core + cs) & 1) * 64, 64)
-            w[pl.ds(row, 64), :] = part[first + cs * 64 : first + cs * 64 + 64, :]
+    copies = []
+
+    def bring(src, dst):
+        copies.append(pltpu.make_async_copy(src, dst, sems.at[len(copies)]))
+        copies[-1].start()
 
     for slot in range(4):
-        place(mine, slot * 128, slot, 0)
-        place(ahead, slot * 128, slot, 1)
-        place(behind, slot * 128, slot, 3)
-        place((far_low, far_high)[slot // 2], (slot % 2) * 128, slot, 2)
-    cots[0] = c_own[0]
-    cots[1] = c_z[0]
-    cots[2] = c_core[0]
-    cots[3] = c_core[1]
+        for dist in range(4):
+            yy = (y + dist + core * (slot - dist)) & 3
+            xx = (x + slot + core * (dist - slot)) & 3
+            for cs in range(2):
+                row = pl.multiple_of((yy * 4 + xx) * 128 + ((core + cs) & 1) * 64, 64)
+                start = (slot % 2) * 128 + cs * 64
+                bring(parts[dist][slot // 2].at[pl.ds(start, 64)], w.at[pl.ds(row, 64)])
+    for blk in range(4):
+        bring(refs[blk], toks.at[blk])
+    for blk, src in enumerate((c_own.at[0], c_z.at[0], c_core.at[0], c_core.at[1])):
+        bring(src, cots.at[blk])
+    for copy in copies:
+        copy.wait()
 
     @pl.loop(0, 3)
     def _(part):
         cols = pl.ds(pl.multiple_of(part * 256, 256), 256)
         for blk in range(4):
-            qkv[blk, :, cols] = dot(toks[blk][...], w[:, cols], 1, 0).astype(BF)
+            qkv[blk, :, cols] = dot(toks[blk], w[:, cols], 1, 0).astype(BF)
 
     @pl.loop(0, 4)
     def _(step):
@@ -257,12 +278,12 @@
         gradient_pair(pos, toks, grads, 2, first, store)
 
 
-def gradient_kernel(pos, t0, t1, t2, t3, grads, own, onward, backward):
+def gradient_kernel(dists, pos, t0, t1, t2, t3, grads, _, *outs):
     toks = (t0, t1, t2, t3)
 
     @pl.loop(0, 2)
     def _(pair):
-        for dist, out in ((1, onward), (3, backward), (0, own)):
+        for dist, out in zip(dists, outs):
 
             def store(sub, rows, value, out=out):
                 out[pair * 2 + sub, rows, :] = value
@@ -270,15 +291,25 @@
             gradient_pair(pos, toks, grads, dist, pair * 2, store)
 
 
-def place_kernel(pos, own, from_core, from_z, mine, near, theirs, attn_out, grad_w):
+def total_kernel(pos, own, r1, r2, attn, from_core, from_z, t0, t1, t2, t3, attn_out):
     core, kind = pos[2], pos[4]
-    attns = ((own, from_z.at[0]), (from_core.at[0], from_z.at[1]))
+    for slot, out in enumerate((t0, t1, t2, t3)):
+        total = own[slot].astype(F32) + r1[slot].astype(F32) + r2[slot].astype(F32)
+        out[...] = total.astype(BF)
+    attns = ((attn.at[0], from_z.at[0]), (from_core.at[0], from_z.at[1]))
+    for cs in range(2):
+        for zs in range(2):
+            group = ((core + cs) & 1) * 2 + ((kind + zs) & 1)
+            attn_out[:, pl.ds(pl.multiple_of(group * 256, 256), 256)] = attns[cs][zs][...]
+
+
+def place_kernel(pos, mine, near, theirs, grad_w):
+    core, kind = pos[2], pos[4]
     halves = (pos[5], pos[6])
     for cs in range(2):
         for zs in range(2):
             group = ((core + cs) & 1) * 2 + ((kind + zs) & 1)
             lane = pl.ds(pl.multiple_of(group * 256, 256), 256)
-            attn_out[:, lane] = attns[cs][zs][0] if zs == 0 and cs == 0 else attns[cs][zs][...]
             for piece in range(2):
                 part = (mine, near)[piece] if zs == 0 else theirs.at[piece]
                 row = pl.ds(pl.multiple_of(((halves[zs] + piece) & 1) * 32, 32), 32)
@@ -313,16 +344,20 @@
         [pos, jnp.transpose(w_qkv, (1, 0, 2))],
         1,
         [((64, COLS), BF), ((64, COLS), BF)],
+        scratch=[pltpu.SemaphoreType.DMA((6,))],
         grant=48,
         nbytes=MIB,
+        n_any=1,
     )
 
     chunk = jnp.concatenate([w_own, swap(w_core, "core", 2, 1)], axis=0)
-    mine = jnp.concatenate([chunk] + [ring(chunk, 0, step) for step in (1, 2, 3)], axis=0)
-    ahead, behind = ring(mine, 1, 1), ring(mine, 1, 3)
-    far_low, far_high = ring(behind[:256], 1, 3), ring(ahead[256:], 1, 1)
-
-    tok01 = swap(inputs, "dp", 8, 1)
+    near = [chunk] + [ring(chunk, 0, step) for step in (1, 2, 3)]
+    mine = [jnp.concatenate(near[:2], axis=0), jnp.concatenate(near[2:], axis=0)]
+    ahead = [ring(part, 1, 1) for part in mine]
+    behind = [ring(part, 1, 3) for part in mine]
+    far = [ring(behind[0], 1, 3), ring(ahead[1], 1, 1)]
+
+    tok01 = hold(swap(inputs, "dp", 8, 1), *far)
     c_own, c_z = call(
         split_kernel,
         [pos, after(cotangent[0], chunk)],
@@ -332,9 +367,9 @@
         nbytes=MIB,
     )
     from_z = swap(c_z, "dp", 8, 1)
-    tok10 = swap(after(inputs, mine), "core", 2, 1)
-    tok11 = swap(after(tok01, behind), "core", 2, 1)
-    to_core = jnp.stack([c_own[1], after(from_z, behind)[1]], axis=0)
+    tok10 = swap(after(inputs, *mine), "core", 2, 1)
+    tok11 = swap(tok01, "core", 2, 1)
+    to_core = jnp.stack([c_own[1], from_z[1]], axis=0)
     c_core = swap(to_core, "core", 2, 1)
     toks = [inputs, tok01, tok10, tok11]
 
@@ -342,7 +377,7 @@
     wide = (4, 2, HEAD, HEAD)
     qkv, cots, s1, x0, g1, m2, m3, m4, m5 = call(
         project_kernel,
-        scalars + toks + [c_own, from_z, c_core, mine, ahead, behind, far_low, far_high],
+        scalars + toks + [c_own, from_z, c_core] + mine + ahead + behind + far,
         3,
         [
             ((4, BLOCK, COLS), BF),
@@ -355,10 +390,15 @@
             (square, BF),
             (square, BF),
         ],
-        scratch=[pltpu.VMEM((D, COLS), BF)],
-        grant=48,
+        scratch=[
+            pltpu.VMEM((D, COLS), BF),
+            pltpu.VMEM((4, BLOCK, D), BF),
+            pltpu.SemaphoreType.DMA((40,)),
+        ],
+        grant=52,
         flops=2 * 1024 * D * COLS,
         nbytes=10 * MIB,
+        n_any=15,
     )
 
     cx = [swap(x0, "x", 4, mask) for mask in (1, 2, 3)]
@@ -394,20 +434,39 @@
         nbytes=12 * MIB,
     )
     low, high = ring(low, 1, 3), ring(high, 1, 1)
-    own, onward, backward = call(
-        gradient_kernel,
-        [pos] + toks + [grads],
-        1,
-        [((4, 128, COLS), BF)] * 3,
-        grant=24,
-        flops=2 * 1024 * D * COLS,
+    from_core = swap(attn[2:], "core", 2, 1)
+    onward, backward = call(
+        functools.partial(gradient_kernel, (1, 3)),
+        [pos] + toks + [grads, from_core],
+        1,
+        [((4, 128, COLS), BF)] * 2,
+        grant=20,
+        flops=1024 * D * COLS,
         nbytes=9 * MIB,
+        n_any=1,
     )
     onward = jnp.concatenate([add(onward[:2], low), onward[2:]], axis=0)
     backward = jnp.concatenate([backward[:2], add(backward[2:], high)], axis=0)
-    from_core = swap(attn[2:], "core", 2, 1)
-    total = add(own, ring(onward, 1, 3), ring(backward, 1, 1))
+    onward, backward = ring(onward, 1, 3), ring(backward, 1, 1)
     back = swap(jnp.stack([attn[1], from_core[1]], axis=0), "dp", 8, 1)
+    (own,) = call(
+        functools.partial(gradient_kernel, (0,)),
+        [pos] + toks + [grads, from_core],
+        1,
+        [((4, 128, COLS), BF)],
+        grant=20,
+        flops=1024 * 512 * COLS,
+        nbytes=9 * MIB,
+        n_any=1,
+    )
+    *total, attn_out = call(
+        total_kernel,
+        [pos, own, onward, backward, attn, from_core, back],
+        1,
+        [((128, COLS), BF)] * 4 + [((BLOCK, 1024), BF)],
+        grant=10,
+        nbytes=4 * MIB,
+    )
     chip_sum = add(total[0], *[ring(total[step], 0, -step) for step in (1, 2, 3)])
     pair = jnp.stack([chip_sum[:64], swap(chip_sum[64:], "core", 2, 1)], axis=0)
     mine = add(pair[:, :32], same_set_neighbour(pair[:, 32:]))
@@ -415,11 +474,11 @@
     near = same_set_neighbour(mine)
     theirs = swap(jnp.stack([mine, near], axis=0), "dp", 8, 1)
 
-    attn_out, grad_w = call(
+    (grad_w,) = call(
         place_kernel,
-        [pos, attn, from_core, back, mine, near, theirs],
-        1,
-        [((BLOCK, 1024), BF), ((3, 64, 1024), F32)],
+        [pos, mine, near, theirs],
+        1,
+        [((3, 64, 1024), F32)],
         grant=6,
         nbytes=3 * MIB,
     )

time: 165 us -> 165 us (level)
  starting transfers between devices: 48.4 us -> 60.5 us
  waiting for transfers between devices: 77.6 us -> 65.8 us
  Pallas kernels: 26.3 us -> 28.7 us
  local copies, waits for them, and re-layouts: 9.37 us -> 7.51 us
    ppermute x14 -> x16, starting transfers between devices: 20.9 us -> 28.9 us  [ring(): return lax.ppermute(value, ('y', 'x', 'core'), pairs)]
    ppermute x14 -> x16, waiting for transfers between devices: 33.2 us -> 26.9 us  [ring(): return lax.ppermute(value, ('y', 'x', 'core'), pairs)]
    ppermute x24, waiting for transfers between devices: 32 us -> 26.8 us  [swap(): return lax.ppermute(value, axis, [(i, i ^ mask) for i in range(size)])]
    ppermute x24, starting transfers between devices: 17.6 us -> 21.1 us  [swap(): return lax.ppermute(value, axis, [(i, i ^ mask) for i in range(size)])]
    slice x4 -> x2, local copies, waits for them, and re-layouts: 4.46 us -> 0.92 us  [per_device(): to_core = jnp.stack([c_own[1], from_z[1]], axis=0)]
    unnamed x26 -> x43, local copies, waits for them, and re-layouts: 3.24 us -> 6.27 us
    pallas_call x7 -> x9, Pallas kernels: 26.3 us -> 28.7 us  [call(): pl.pallas_call(kernel, out_shape=[jax.ShapeDtypeStruct(*out) for out in o...]
  transfers between devices with their start and end apart: 41 -> 43, of which waited for: 22 -> 22; matrix products, arithmetic and copies ran while one was open for 5% -> 2% of each run, Pallas kernels for 6% -> 7%
where the time goes in v1:
time: 165 us
  waiting for transfers between devices  65.8 us (40%)
  starting transfers between devices  60.5 us (37%)
  Pallas kernels  28.7 us (17%)
  local copies, waits for them, and re-layouts  7.51 us (5%)
    ppermute x16, starting transfers between devices, ring(): return lax.ppermute(value, ('y', 'x', 'core'), pairs)  28.9 us
    pallas_call x9, Pallas kernels, call(): pl.pallas_call(kernel, out_shape=[jax.ShapeDtypeStruct(*out) for out in o...  28.7 us
    ppermute x16, waiting for transfers between devices, ring(): return lax.ppermute(value, ('y', 'x', 'core'), pairs)  26.9 us
    ppermute x24, waiting for transfers between devices, swap(): return lax.ppermute(value, axis, [(i, i ^ mask) for i in range(size)])  26.8 us
    ppermute x24, starting transfers between devices, swap(): return lax.ppermute(value, axis, [(i, i ^ mask) for i in range(size)])  21.1 us
    ppermute x2, starting transfers between devices, same_set_neighbour(): lax.ppermute(value, 'dp', [(z, (z + 1 if z % 2 else z - 1) % 8) for z in...  8.56 us
    unnamed x43, local copies, waits for them, and re-layouts  6.27 us
    ppermute x1, waiting for transfers between devices, same_set_far(): lax.ppermute(value, 'dp', [(z, ((7 if SETS >> z & 1 else 3) - z) % 8) for...  6.06 us
  transfers between devices with their start and end apart: 43, of which 22 were waited for; matrix products, arithmetic and copies ran while one was open for 2% of the time, Pallas kernels for 7%

profile of v1, /device:TPU:6, one launch (start us, length us, event | category | flops | bytes accessed | tf_op | source)
XLA Modules:
  0.0 165.1 jit_solution(7162486052644178687)
XLA Ops:
  4.8 2.8 %collective-permute-start.5 = (bf16[128,768]{1,0:T(8,128)(2,1)S(1)}, bf16[128,768]{1,0:T(8,128)(2,1)S(1)}, u32[]{:S(2)}, u32[]{:S(2)}) collective-permute-start(bf16[128,768]{1,0:T(8,128)(2,1)S(1)} %get-tuple-element.59), channel_id=1, source_target_pairs={{0,32},{8,136},{16,48},{24,152},{32,0},{40,168},{48,16},{56,184},{... | collective-permute-start | bytes 589832 | tf_op jit(solution)/shard_map/ppermute | solution.py:30
  7.8 2.1 %collective-permute-start.6 = (bf16[128,768]{1,0:T(8,128)(2,1)S(1)}, bf16[128,768]{1,0:T(8,128)(2,1)S(1)}, u32[]{:S(2)}, u32[]{:S(2)}) collective-permute-start(bf16[128,768]{1,0:T(8,128)(2,1)S(1)} %get-tuple-element.59), channel_id=1, source_target_pairs={{0,16},{8,72},{16,32},{24,88},{32,48},{40,104},{48,0},{56,120},{64... | collective-permute-start | bytes 589832 | tf_op jit(solution)/shard_map/ppermute | solution.py:30
  10.9 3.8 %collective-permute-start.3 = (bf16[256,768]{1,0:T(8,128)(2,1)S(1)}, bf16[256,768]{1,0:T(8,128)(2,1)S(1)}, u32[]{:S(2)}, u32[]{:S(2)}) collective-permute-start(bf16[256,768]{1,0:T(8,128)(2,1)S(1)} %constant_dynamic-update-slice_fusion.2.refs_7_), channel_id=1, source_target_pairs={{0,64},{8,24},{16,80},{24,40},{32,96},{40,56},{48,112},{56,8},{64,... | collective-permute-start | bytes 1179656 | tf_op jit(solution)/shard_map/ppermute | solution.py:30
  14.7 2.2 %collective-permute-start.7 = (bf16[256,768]{1,0:T(8,128)(2,1)S(1)}, bf16[256,768]{1,0:T(8,128)(2,1)S(1)}, u32[]{:S(2)}, u32[]{:S(2)}) collective-permute-start(bf16[256,768]{1,0:T(8,128)(2,1)S(1)} %constant_dynamic-update-slice_fusion.5.refs_8_), channel_id=1, source_target_pairs={{0,192},{8,56},{16,208},{24,8},{32,224},{40,24},{48,240},{56,40},{... | collective-permute-start | bytes 1179656 | tf_op jit(solution)/shard_map/ppermute | solution.py:30
  16.9 4.9 %collective-permute-done.3.refs_11_ = bf16[256,768]{1,0:T(8,128)(2,1)S(1)} collective-permute-done((bf16[256,768]{1,0:T(8,128)(2,1)S(1)}, bf16[256,768]{1,0:T(8,128)(2,1)S(1)}, u32[]{:S(2)}, u32[]{:S(2)}) %collective-permute-start.3) | collective-permute-done | bytes 393248 | tf_op jit(solution)/shard_map/ppermute | solution.py:30
  22.7 3.3 %collective-permute-start.8 = (bf16[256,768]{1,0:T(8,128)(2,1)S(1)}, bf16[256,768]{1,0:T(8,128)(2,1)}, u32[]{:S(2)}, u32[]{:S(2)}) collective-permute-start(bf16[256,768]{1,0:T(8,128)(2,1)S(1)} %collective-permute-done.7.refs_10_), channel_id=1, source_target_pairs={{0,192},{8,56},{16,208},{24,8},{32,224},{40,24},{48,240},{56,40},{... | collective-permute-start | bytes 1179656 | tf_op jit(solution)/shard_map/ppermute | solution.py:30
  25.9 6.7 %collective-permute-done.refs_0_ = bf16[256,2048]{1,0:T(8,128)(2,1)S(1)} collective-permute-done((bf16[256,2048]{1,0:T(8,128)(2,1)}, bf16[256,2048]{1,0:T(8,128)(2,1)S(1)}, u32[]{:S(2)}, u32[]{:S(2)}) %collective-permute-start) | collective-permute-done | bytes 1048608 | tf_op jit(solution)/shard_map/ppermute | solution.py:34
  39.5 5.5 %collective-permute-done.11 = s32[1,12]{1,0:T(1,128)S(1)} collective-permute-done((s32[1,12]{1,0:T(1,128)S(1)}, s32[1,12]{1,0:T(1,128)S(1)}, u32[]{:S(2)}, u32[]{:S(2)}) %collective-permute-start.11) | collective-permute-done | bytes 80 | tf_op jit(solution)/shard_map/ppermute | solution.py:34
  49.8 4.5 %collective-permute-done.16.refs_12_ = bf16[256,768]{1,0:T(8,128)(2,1)} collective-permute-done((bf16[256,768]{1,0:T(8,128)(2,1)}, bf16[256,768]{1,0:T(8,128)(2,1)}, u32[]{:S(2)}, u32[]{:S(2)}) %collective-permute-start.16) | collective-permute-done | bytes 393248 | tf_op jit(solution)/shard_map/ppermute | solution.py:30
  56.3 10.8 %shard_map.71 = (bf16[4,256,768]{2,1,0:T(8,128)(2,1)}, bf16[4,256,256]{2,1,0:T(8,128)(2,1)}, bf16[4,2,128,128]{3,2,1,0:T(8,128)(2,1)S(1)}, bf16[2,2,128,128]{3,2...) custom-call(s32[7]{0:T(128)S(1)} %stack.55.pos, ...), custom_call_target="tpu_custom_call" | custom-call | flops 3221225472 | bytes 10485760 | tf_op jit(solution)/shard_map/pallas_call | solution.py:73
  67.2 2.2 %collective-permute-start.25 = (bf16[2,2,128,128]{3,2,1,0:T(8,128)(2,1)S(1)}, bf16[2,2,128,128]{3,2,1,0:T(8,128)(2,1)S(1)}, u32[]{:S(2)}, u32[]{:S(2)}) collective-permute-start(bf16[2,2,128,128]{3,2,1,0:T(8,128)(2,1)S(1)} %get-tuple-element.40), channel_id=1, source_target_pairs={{0,192},{64,128},{128,64},{192,0},{1,193},{65,129},{129,65},{193,1... | collective-permute-start | bytes 393224 | tf_op jit(solution)/shard_map/ppermute | solution.py:34
  76.3 2.0 %collective-permute-start.28 = (bf16[2,2,128,128]{3,2,1,0:T(8,128)(2,1)S(1)}, bf16[2,2,128,128]{3,2,1,0:T(8,128)(2,1)S(1)}, u32[]{:S(2)}, u32[]{:S(2)}) collective-permute-start(bf16[2,2,128,128]{3,2,1,0:T(8,128)(2,1)S(1)} %get-tuple-element.54), channel_id=1, source_target_pairs={{0,48},{16,32},{32,16},{48,0},{1,49},{17,33},{33,17},{49,1},{2,50}... | collective-permute-start | bytes 393224 | tf_op jit(solution)/shard_map/ppermute | solution.py:34
  82.0 2.3 %collective-permute-start.21 = (bf16[2,2,128,128]{3,2,1,0:T(8,128)(2,1)S(1)}, bf16[2,2,128,128]{3,2,1,0:T(8,128)(2,1)S(1)}, u32[]{:S(2)}, u32[]{:S(2)}) collective-permute-start(bf16[2,2,128,128]{3,2,1,0:T(8,128)(2,1)S(1)} %add_convert_fusion.5), channel_id=1, source_target_pairs={{0,128},{64,192},{128,0},{192,64},{1,129},{65,193},{129,1},{193,65... | collective-permute-start | bytes 393224 | tf_op jit(solution)/shard_map/ppermute | solution.py:34
  86.5 5.1 %shard_map.72.refs_6_ = f32[4,256,1024]{2,1,0:T(8,128)S(1)} custom-call(s32[7]{0:T(128)S(1)} %stack.55.pos, s32[4,12]{1,0:T(4,128)S(1)} %pad_add_fusion.idx, f32[16,8]{1,0:T(8,128)S(1)} %copy.10.table, bf16[4,256,768]{2,1,0:T(8,128)(2,1)S(1)} %copy-done.8, bf16[4,256,256]{2,1,0:T(8,128)(2,1)S(1)} %copy-done.9), custom_call_target="tpu_custom_call" | custom-call | flops 805306368 | bytes 8388608 | tf_op jit(solution)/shard_map/pallas_call | solution.py:73
  91.8 3.4 %shard_map.73 = (bf16[4,256,256]{2,1,0:T(8,128)(2,1)S(1)}, bf16[4,256,768]{2,1,0:T(8,128)(2,1)S(1)}, bf16[2,128,768]{2,1,0:T(8,128)(2,1)S(1)}, bf16[2,128,768]{2,1,0:T(8,128)(2,1)S(1)}) custom-call(s32[7]{0:T(128)S(1)} %stack.55.pos, s32[4,12]{1,0:T(4,128)S(1)} %pad_add_fusion.idx, f32[16,8]{1,0:T(8,128)S(1)} %copy.10.table, bf16[256,2048]{1,0:T(8,128)(2,1)S(1)} %bitcast.20, ...), custom_call_target="tpu_custom_call" | custom-call | flops 1610612736 | bytes 12582912 | tf_op jit(solution)/shard_map/pallas_call | solution.py:73
  95.2 4.2 %collective-permute-start.32 = (bf16[2,128,768]{2,1,0:T(8,128)(2,1)S(1)}, bf16[2,128,768]{2,1,0:T(8,128)(2,1)S(1)}, u32[]{:S(2)}, u32[]{:S(2)}) collective-permute-start(bf16[2,128,768]{2,1,0:T(8,128)(2,1)S(1)} %get-tuple-element.48), channel_id=1, source_target_pairs={{0,192},{8,56},{16,208},{24,8},{32,224},{40,24},{48,240},{56,40},{... | collective-permute-start | bytes 1179656 | tf_op jit(solution)/shard_map/ppermute | solution.py:30
  99.4 2.6 %shard_map.75 = (bf16[4,128,768]{2,1,0:T(8,128)(2,1)S(1)}, bf16[4,128,768]{2,1,0:T(8,128)(2,1)S(1)}) custom-call(s32[7]{0:T(128)S(1)} %stack.55.pos, bf16[256,2048]{1,0:T(8,128)(2,1)S(1)} %bitcast.21, bf16[256,2048]{1,0:T(8,128)(2,1)S(1)} %copy-done.1, bf16[256,2048]{1,0:T(8,128)(2,1)S(1)} %copy-done.5, bf16[256,2048]{1,0:T(8,128)(2,1)S(1)} %copy-done.7, ...), custom_call_target="tpu_custom_call" | custom-call | flops 1610612736 | bytes 9437184 | tf_op jit(solution)/shard_map/pallas_call | solution.py:73
  102.2 2.6 %collective-permute-done.32 = bf16[2,128,768]{2,1,0:T(8,128)(2,1)S(1)} collective-permute-done((bf16[2,128,768]{2,1,0:T(8,128)(2,1)S(1)}, bf16[2,128,768]{2,1,0:T(8,128)(2,1)S(1)}, u32[]{:S(2)}, u32[]{:S(2)}) %collective-permute-start.32) | collective-permute-done | bytes 393248 | tf_op jit(solution)/shard_map/ppermute | solution.py:30
  104.9 3.8 %collective-permute-start.33 = (bf16[4,128,768]{2,1,0:T(8,128)(2,1)S(1)}, bf16[4,128,768]{2,1,0:T(8,128)(2,1)S(1)}, u32[]{:S(2)}, u32[]{:S(2)}) collective-permute-start(bf16[4,128,768]{2,1,0:T(8,128)(2,1)S(1)} %pad_maximum_fusion.1), channel_id=1, source_target_pairs={{0,192},{8,56},{16,208},{24,8},{32,224},{40,24},{48,240},{56,40},{... | collective-permute-start | bytes 2359304 | tf_op jit(solution)/shard_map/ppermute | solution.py:30
  112.4 3.1 %collective-permute-done.34.from_z = bf16[2,256,256]{2,1,0:T(8,128)(2,1)S(1)} collective-permute-done((bf16[2,256,256]{2,1,0:T(8,128)(2,1)S(1)}, bf16[2,256,256]{2,1,0:T(8,128)(2,1)S(1)}, u32[]{:S(2)}, u32[]{:S(2)}) %collective-permute-start.34) | collective-permute-done | bytes 262176 | tf_op jit(solution)/shard_map/ppermute | solution.py:34
  115.5 2.7 %collective-permute-done.33.r2 = bf16[4,128,768]{2,1,0:T(8,128)(2,1)S(1)} collective-permute-done((bf16[4,128,768]{2,1,0:T(8,128)(2,1)S(1)}, bf16[4,128,768]{2,1,0:T(8,128)(2,1)S(1)}, u32[]{:S(2)}, u32[]{:S(2)}) %collective-permute-start.33) | collective-permute-done | bytes 786464 | tf_op jit(solution)/shard_map/ppermute | solution.py:30
  118.2 4.0 %collective-permute-done.31.r1 = bf16[4,128,768]{2,1,0:T(8,128)(2,1)S(1)} collective-permute-done((bf16[4,128,768]{2,1,0:T(8,128)(2,1)S(1)}, bf16[4,128,768]{2,1,0:T(8,128)(2,1)S(1)}, u32[]{:S(2)}, u32[]{:S(2)}) %collective-permute-start.31) | collective-permute-done | bytes 786464 | tf_op jit(solution)/shard_map/ppermute | solution.py:30
  126.5 2.9 %collective-permute-done.35 = bf16[128,768]{1,0:T(8,128)(2,1)S(1)} collective-permute-done((bf16[128,768]{1,0:T(8,128)(2,1)S(1)}, bf16[128,768]{1,0:T(8,128)(2,1)S(1)}, u32[]{:S(2)}, u32[]{:S(2)}) %collective-permute-start.35) | collective-permute-done | bytes 196640 | tf_op jit(solution)/shard_map/ppermute | solution.py:30
  129.4 2.2 %collective-permute-done.36 = bf16[128,768]{1,0:T(8,128)(2,1)S(1)} collective-permute-done((bf16[128,768]{1,0:T(8,128)(2,1)S(1)}, bf16[128,768]{1,0:T(8,128)(2,1)S(1)}, u32[]{:S(2)}, u32[]{:S(2)}) %collective-permute-start.36) | collective-permute-done | bytes 196640 | tf_op jit(solution)/shard_map/ppermute | solution.py:30
  131.6 2.0 %collective-permute-done.37 = bf16[128,768]{1,0:T(8,128)(2,1)S(1)} collective-permute-done((bf16[128,768]{1,0:T(8,128)(2,1)S(1)}, bf16[128,768]{1,0:T(8,128)(2,1)S(1)}, u32[]{:S(2)}, u32[]{:S(2)}) %collective-permute-start.37) | collective-permute-done | bytes 196640 | tf_op jit(solution)/shard_map/ppermute | solution.py:30
  135.2 5.6 %collective-permute-start.39 = (bf16[2,32,768]{2,1,0:T(8,128)(2,1)S(1)}, bf16[2,32,768]{2,1,0:T(8,128)(2,1)S(1)}, u32[]{:S(2)}, u32[]{:S(2)}) collective-permute-start(bf16[2,32,768]{2,1,0:T(8,128)(2,1)S(1)} %pad_maximum_fusion.5), channel_id=1, source_target_pairs={{0,7},{1,2},{2,1},{3,4},{4,3},{5,6},{6,5},{7,0},{8,15},{9,10},{10,... | collective-permute-start | bytes 294920 | tf_op jit(solution)/shard_map/ppermute | solution.py:38
  140.8 3.1 %collective-permute-done.39 = bf16[2,32,768]{2,1,0:T(8,128)(2,1)S(1)} collective-permute-done((bf16[2,32,768]{2,1,0:T(8,128)(2,1)S(1)}, bf16[2,32,768]{2,1,0:T(8,128)(2,1)S(1)}, u32[]{:S(2)}, u32[]{:S(2)}) %collective-permute-start.39) | collective-permute-done | bytes 98336 | tf_op jit(solution)/shard_map/ppermute | solution.py:38
  143.9 2.0 %collective-permute-start.40 = (bf16[2,32,768]{2,1,0:T(8,128)(2,1)S(1)}, bf16[2,32,768]{2,1,0:T(8,128)(2,1)S(1)}, u32[]{:S(2)}, u32[]{:S(2)}) collective-permute-start(bf16[2,32,768]{2,1,0:T(8,128)(2,1)S(1)} %add_convert_fusion.7), channel_id=1, source_target_pairs={{0,3},{1,6},{2,5},{3,0},{4,7},{5,2},{6,1},{7,4},{8,11},{9,14},{10,... | collective-permute-start | bytes 294920 | tf_op jit(solution)/shard_map/ppermute | solution.py:42
  145.8 6.1 %collective-permute-done.40 = bf16[2,32,768]{2,1,0:T(8,128)(2,1)S(1)} collective-permute-done((bf16[2,32,768]{2,1,0:T(8,128)(2,1)S(1)}, bf16[2,32,768]{2,1,0:T(8,128)(2,1)S(1)}, u32[]{:S(2)}, u32[]{:S(2)}) %collective-permute-start.40) | collective-permute-done | bytes 98336 | tf_op jit(solution)/shard_map/ppermute | solution.py:42
  152.0 2.9 %collective-permute-start.41 = (bf16[2,32,768]{2,1,0:T(8,128)(2,1)S(1)}, bf16[2,32,768]{2,1,0:T(8,128)(2,1)S(1)}, u32[]{:S(2)}, u32[]{:S(2)}) collective-permute-start(bf16[2,32,768]{2,1,0:T(8,128)(2,1)S(1)} %add_convert_fusion.6.mine), channel_id=1, source_target_pairs={{0,7},{1,2},{2,1},{3,4},{4,3},{5,6},{6,5},{7,0},{8,15},{9,10},{10,... | collective-permute-start | bytes 294920 | tf_op jit(solution)/shard_map/ppermute | solution.py:38
  154.9 3.0 %collective-permute-done.41.near = bf16[2,32,768]{2,1,0:T(8,128)(2,1)S(1)} collective-permute-done((bf16[2,32,768]{2,1,0:T(8,128)(2,1)S(1)}, bf16[2,32,768]{2,1,0:T(8,128)(2,1)S(1)}, u32[]{:S(2)}, u32[]{:S(2)}) %collective-permute-start.41) | collective-permute-done | bytes 98336 | tf_op jit(solution)/shard_map/ppermute | solution.py:38
  158.0 5.7 %collective-permute-done.42.theirs = bf16[2,2,32,768]{3,2,1,0:T(8,128)(2,1)S(1)} collective-permute-done((bf16[2,2,32,768]{3,2,1,0:T(8,128)(2,1)S(1)}, bf16[2,2,32,768]{3,2,1,0:T(8,128)(2,1)S(1)}, u32[]{:S(2)}, u32[]{:S(2)}) %collective-permute-start.42) | collective-permute-done | bytes 196640 | tf_op jit(solution)/shard_map/ppermute | solution.py:34
  (135 shorter events, 44.1 us)
Async XLA Ops:
  3.9 7.0 %collective-permute-start.2 = (bf16[128,768]{1,0:T(8,128)(2,1)S(1)}, bf16[128,768]{1,0:T(8,128)(2,1)S(1)}, u32[]{:S(2)}, u32[]{:S(2)}) collective-permute-start(bf16[128,768]{1,0:T(8,128)(2,1)S(1)} %get-tuple-element.59), channel_id=1, source_target_pairs={{0,48},{8,200},{16,0},{24,216},{32,16},{40,232},{48,32},{56,248},{... | collective-permute-start | bytes 589832 | tf_op jit(solution)/shard_map/ppermute | solution.py:30
  4.8 9.8 %collective-permute-start.5 = (bf16[128,768]{1,0:T(8,128)(2,1)S(1)}, bf16[128,768]{1,0:T(8,128)(2,1)S(1)}, u32[]{:S(2)}, u32[]{:S(2)}) collective-permute-start(bf16[128,768]{1,0:T(8,128)(2,1)S(1)} %get-tuple-element.59), channel_id=1, source_target_pairs={{0,32},{8,136},{16,48},{24,152},{32,0},{40,168},{48,16},{56,184},{... | collective-permute-start | bytes 589832 | tf_op jit(solution)/shard_map/ppermute | solution.py:30
  7.6 25.0 %collective-permute-start = (bf16[256,2048]{1,0:T(8,128)(2,1)}, bf16[256,2048]{1,0:T(8,128)(2,1)S(1)}, u32[]{:S(2)}, u32[]{:S(2)}) collective-permute-start(bf16[256,2048]{1,0:T(8,128)(2,1)} %bitcast.17), channel_id=1, source_target_pairs={{0,1},{1,0},{2,3},{3,2},{4,5},{5,4},{6,7},{7,6},{8,9},{9,8},{10,11... | collective-permute-start | bytes 3145736 | tf_op jit(solution)/shard_map/ppermute | solution.py:34
  7.8 6.8 %collective-permute-start.6 = (bf16[128,768]{1,0:T(8,128)(2,1)S(1)}, bf16[128,768]{1,0:T(8,128)(2,1)S(1)}, u32[]{:S(2)}, u32[]{:S(2)}) collective-permute-start(bf16[128,768]{1,0:T(8,128)(2,1)S(1)} %get-tuple-element.59), channel_id=1, source_target_pairs={{0,16},{8,72},{16,32},{24,88},{32,48},{40,104},{48,0},{56,120},{64... | collective-permute-start | bytes 589832 | tf_op jit(solution)/shard_map/ppermute | solution.py:30
  10.9 11.0 %collective-permute-start.3 = (bf16[256,768]{1,0:T(8,128)(2,1)S(1)}, bf16[256,768]{1,0:T(8,128)(2,1)S(1)}, u32[]{:S(2)}, u32[]{:S(2)}) collective-permute-start(bf16[256,768]{1,0:T(8,128)(2,1)S(1)} %constant_dynamic-update-slice_fusion.2.refs_7_), channel_id=1, source_target_pairs={{0,64},{8,24},{16,80},{24,40},{32,96},{40,56},{48,112},{56,8},{64,... | collective-permute-start | bytes 1179656 | tf_op jit(solution)/shard_map/ppermute | solution.py:30
  14.7 7.9 %collective-permute-start.7 = (bf16[256,768]{1,0:T(8,128)(2,1)S(1)}, bf16[256,768]{1,0:T(8,128)(2,1)S(1)}, u32[]{:S(2)}, u32[]{:S(2)}) collective-permute-start(bf16[256,768]{1,0:T(8,128)(2,1)S(1)} %constant_dynamic-update-slice_fusion.5.refs_8_), channel_id=1, source_target_pairs={{0,192},{8,56},{16,208},{24,8},{32,224},{40,24},{48,240},{56,40},{... | collective-permute-start | bytes 1179656 | tf_op jit(solution)/shard_map/ppermute | solution.py:30
  21.8 10.8 %collective-permute-start.4 = (bf16[256,768]{1,0:T(8,128)(2,1)S(1)}, bf16[256,768]{1,0:T(8,128)(2,1)}, u32[]{:S(2)}, u32[]{:S(2)}) collective-permute-start(bf16[256,768]{1,0:T(8,128)(2,1)S(1)} %collective-permute-done.3.refs_11_), channel_id=1, source_target_pairs={{0,64},{8,24},{16,80},{24,40},{32,96},{40,56},{48,112},{56,8},{64,... | collective-permute-start | bytes 1179656 | tf_op jit(solution)/shard_map/ppermute | solution.py:30
  22.7 10.0 %collective-permute-start.8 = (bf16[256,768]{1,0:T(8,128)(2,1)S(1)}, bf16[256,768]{1,0:T(8,128)(2,1)}, u32[]{:S(2)}, u32[]{:S(2)}) collective-permute-start(bf16[256,768]{1,0:T(8,128)(2,1)S(1)} %collective-permute-done.7.refs_10_), channel_id=1, source_target_pairs={{0,192},{8,56},{16,208},{24,8},{32,224},{40,24},{48,240},{56,40},{... | collective-permute-start | bytes 1179656 | tf_op jit(solution)/shard_map/ppermute | solution.py:30
  25.9 28.4 %collective-permute-start.9 = (bf16[256,2048]{1,0:T(8,128)(2,1)S(1)}, bf16[256,2048]{1,0:T(8,128)(2,1)S(1)}, u32[]{:S(2)}, u32[]{:S(2)}) collective-permute-start(bf16[256,2048]{1,0:T(8,128)(2,1)S(1)} %bitcast.19), channel_id=1, source_target_pairs={{0,8},{8,0},{1,9},{9,1},{2,10},{10,2},{3,11},{11,3},{4,12},{12,4},... | collective-permute-start | bytes 3145736 | tf_op jit(solution)/shard_map/ppermute | solution.py:34
  33.7 20.7 %collective-permute-start.10 = (bf16[256,2048]{1,0:T(8,128)(2,1)}, bf16[256,2048]{1,0:T(8,128)(2,1)S(1)}, u32[]{:S(2)}, u32[]{:S(2)}) collective-permute-start(bf16[256,2048]{1,0:T(8,128)(2,1)} %shard_map.69.refs_1_.t1), channel_id=1, source_target_pairs={{0,8},{8,0},{1,9},{9,1},{2,10},{10,2},{3,11},{11,3},{4,12},{12,4},... | collective-permute-start | bytes 3145736 | tf_op jit(solution)/shard_map/ppermute | solution.py:34
  36.0 10.0 %collective-permute-start.13 = (bf16[2,256,256]{2,1,0:T(8,128)(2,1)}, bf16[2,256,256]{2,1,0:T(8,128)(2,1)}, u32[]{:S(2)}, u32[]{:S(2)}) collective-permute-start(bf16[2,256,256]{2,1,0:T(8,128)(2,1)} %get-tuple-element.33), channel_id=1, source_target_pairs={{0,1},{1,0},{2,3},{3,2},{4,5},{5,4},{6,7},{7,6},{8,9},{9,8},{10,11... | collective-permute-start | bytes 786440 | tf_op jit(solution)/shard_map/ppermute | solution.py:34
  37.3 7.7 %collective-permute-start.11 = (s32[1,12]{1,0:T(1,128)S(1)}, s32[1,12]{1,0:T(1,128)S(1)}, u32[]{:S(2)}, u32[]{:S(2)}) collective-permute-start(s32[1,12]{1,0:T(1,128)S(1)} %reshape.7), channel_id=1, source_target_pairs={{0,1},{1,0},{2,3},{3,2},{4,5},{5,4},{6,7},{7,6},{8,9},{9,8},{10,11... | collective-permute-start | bytes 152 | tf_op jit(solution)/shard_map/ppermute | solution.py:34
  38.1 11.7 %collective-permute-start.15 = (bf16[256,768]{1,0:T(8,128)(2,1)}, bf16[256,768]{1,0:T(8,128)(2,1)}, u32[]{:S(2)}, u32[]{:S(2)}) collective-permute-start(bf16[256,768]{1,0:T(8,128)(2,1)} %copy-done.15), channel_id=1, source_target_pairs={{0,192},{8,56},{16,208},{24,8},{32,224},{40,24},{48,240},{56,40},{... | collective-permute-start | bytes 1179656 | tf_op jit(solution)/shard_map/ppermute | solution.py:30
  45.1 9.3 %collective-permute-start.16 = (bf16[256,768]{1,0:T(8,128)(2,1)}, bf16[256,768]{1,0:T(8,128)(2,1)}, u32[]{:S(2)}, u32[]{:S(2)}) collective-permute-start(bf16[256,768]{1,0:T(8,128)(2,1)} %copy-done.14), channel_id=1, source_target_pairs={{0,64},{8,24},{16,80},{24,40},{32,96},{40,56},{48,112},{56,8},{64,... | collective-permute-start | bytes 1179656 | tf_op jit(solution)/shard_map/ppermute | solution.py:30
  67.1 7.1 %collective-permute-start.23 = (bf16[2,2,128,128]{3,2,1,0:T(8,128)(2,1)S(1)}, bf16[2,2,128,128]{3,2,1,0:T(8,128)(2,1)S(1)}, u32[]{:S(2)}, u32[]{:S(2)}) collective-permute-start(bf16[2,2,128,128]{3,2,1,0:T(8,128)(2,1)S(1)} %get-tuple-element.39), channel_id=1, source_target_pairs={{0,64},{64,0},{128,192},{192,128},{1,65},{65,1},{129,193},{193,129... | collective-permute-start | bytes 393224 | tf_op jit(solution)/shard_map/ppermute | solution.py:34
  67.2 8.9 %collective-permute-start.25 = (bf16[2,2,128,128]{3,2,1,0:T(8,128)(2,1)S(1)}, bf16[2,2,128,128]{3,2,1,0:T(8,128)(2,1)S(1)}, u32[]{:S(2)}, u32[]{:S(2)}) collective-permute-start(bf16[2,2,128,128]{3,2,1,0:T(8,128)(2,1)S(1)} %get-tuple-element.40), channel_id=1, source_target_pairs={{0,192},{64,128},{128,64},{192,0},{1,193},{65,129},{129,65},{193,1... | collective-permute-start | bytes 393224 | tf_op jit(solution)/shard_map/ppermute | solution.py:34
  69.4 6.8 %collective-permute-start.24 = (bf16[2,2,128,128]{3,2,1,0:T(8,128)(2,1)S(1)}, bf16[2,2,128,128]{3,2,1,0:T(8,128)(2,1)S(1)}, u32[]{:S(2)}, u32[]{:S(2)}) collective-permute-start(bf16[2,2,128,128]{3,2,1,0:T(8,128)(2,1)S(1)} %get-tuple-element.40), channel_id=1, source_target_pairs={{0,128},{64,192},{128,0},{192,64},{1,129},{65,193},{129,1},{193,65... | collective-permute-start | bytes 393224 | tf_op jit(solution)/shard_map/ppermute | solution.py:34
  71.3 7.9 %collective-permute-start.19 = (bf16[2,2,128,128]{3,2,1,0:T(8,128)(2,1)S(1)}, bf16[2,2,128,128]{3,2,1,0:T(8,128)(2,1)S(1)}, u32[]{:S(2)}, u32[]{:S(2)}) collective-permute-start(bf16[2,2,128,128]{3,2,1,0:T(8,128)(2,1)S(1)} %get-tuple-element.38), channel_id=1, source_target_pairs={{0,48},{16,32},{32,16},{48,0},{1,49},{17,33},{33,17},{49,1},{2,50}... | collective-permute-start | bytes 393224 | tf_op jit(solution)/shard_map/ppermute | solution.py:34
  72.7 7.7 %collective-permute-start.18 = (bf16[2,2,128,128]{3,2,1,0:T(8,128)(2,1)S(1)}, bf16[2,2,128,128]{3,2,1,0:T(8,128)(2,1)S(1)}, u32[]{:S(2)}, u32[]{:S(2)}) collective-permute-start(bf16[2,2,128,128]{3,2,1,0:T(8,128)(2,1)S(1)} %get-tuple-element.38), channel_id=1, source_target_pairs={{0,32},{16,48},{32,0},{48,16},{1,33},{17,49},{33,1},{49,17},{2,34}... | collective-permute-start | bytes 393224 | tf_op jit(solution)/shard_map/ppermute | solution.py:34
  76.3 15.4 %collective-permute-start.28 = (bf16[2,2,128,128]{3,2,1,0:T(8,128)(2,1)S(1)}, bf16[2,2,128,128]{3,2,1,0:T(8,128)(2,1)S(1)}, u32[]{:S(2)}, u32[]{:S(2)}) collective-permute-start(bf16[2,2,128,128]{3,2,1,0:T(8,128)(2,1)S(1)} %get-tuple-element.54), channel_id=1, source_target_pairs={{0,48},{16,32},{32,16},{48,0},{1,49},{17,33},{33,17},{49,1},{2,50}... | collective-permute-start | bytes 393224 | tf_op jit(solution)/shard_map/ppermute | solution.py:34
  78.3 13.4 %collective-permute-start.27 = (bf16[2,2,128,128]{3,2,1,0:T(8,128)(2,1)S(1)}, bf16[2,2,128,128]{3,2,1,0:T(8,128)(2,1)S(1)}, u32[]{:S(2)}, u32[]{:S(2)}) collective-permute-start(bf16[2,2,128,128]{3,2,1,0:T(8,128)(2,1)S(1)} %get-tuple-element.54), channel_id=1, source_target_pairs={{0,32},{16,48},{32,0},{48,16},{1,33},{17,49},{33,1},{49,17},{2,34}... | collective-permute-start | bytes 393224 | tf_op jit(solution)/shard_map/ppermute | solution.py:34
  80.5 11.1 %collective-permute-start.22 = (bf16[2,2,128,128]{3,2,1,0:T(8,128)(2,1)S(1)}, bf16[2,2,128,128]{3,2,1,0:T(8,128)(2,1)S(1)}, u32[]{:S(2)}, u32[]{:S(2)}) collective-permute-start(bf16[2,2,128,128]{3,2,1,0:T(8,128)(2,1)S(1)} %add_convert_fusion.5), channel_id=1, source_target_pairs={{0,192},{64,128},{128,64},{192,0},{1,193},{65,129},{129,65},{193,1... | collective-permute-start | bytes 393224 | tf_op jit(solution)/shard_map/ppermute | solution.py:34
  82.0 9.7 %collective-permute-start.21 = (bf16[2,2,128,128]{3,2,1,0:T(8,128)(2,1)S(1)}, bf16[2,2,128,128]{3,2,1,0:T(8,128)(2,1)S(1)}, u32[]{:S(2)}, u32[]{:S(2)}) collective-permute-start(bf16[2,2,128,128]{3,2,1,0:T(8,128)(2,1)S(1)} %add_convert_fusion.5), channel_id=1, source_target_pairs={{0,128},{64,192},{128,0},{192,64},{1,129},{65,193},{129,1},{193,65... | collective-permute-start | bytes 393224 | tf_op jit(solution)/shard_map/ppermute | solution.py:34
  95.2 9.5 %collective-permute-start.32 = (bf16[2,128,768]{2,1,0:T(8,128)(2,1)S(1)}, bf16[2,128,768]{2,1,0:T(8,128)(2,1)S(1)}, u32[]{:S(2)}, u32[]{:S(2)}) collective-permute-start(bf16[2,128,768]{2,1,0:T(8,128)(2,1)S(1)} %get-tuple-element.48), channel_id=1, source_target_pairs={{0,192},{8,56},{16,208},{24,8},{32,224},{40,24},{48,240},{56,40},{... | collective-permute-start | bytes 1179656 | tf_op jit(solution)/shard_map/ppermute | solution.py:30
  99.4 9.2 %collective-permute-start.30 = (bf16[2,128,768]{2,1,0:T(8,128)(2,1)S(1)}, bf16[2,128,768]{2,1,0:T(8,128)(2,1)S(1)}, u32[]{:S(2)}, u32[]{:S(2)}) collective-permute-start(bf16[2,128,768]{2,1,0:T(8,128)(2,1)S(1)} %get-tuple-element.46), channel_id=1, source_target_pairs={{0,64},{8,24},{16,80},{24,40},{32,96},{40,56},{48,112},{56,8},{64,... | collective-permute-start | bytes 1179656 | tf_op jit(solution)/shard_map/ppermute | solution.py:30
  104.9 13.3 %collective-permute-start.33 = (bf16[4,128,768]{2,1,0:T(8,128)(2,1)S(1)}, bf16[4,128,768]{2,1,0:T(8,128)(2,1)S(1)}, u32[]{:S(2)}, u32[]{:S(2)}) collective-permute-start(bf16[4,128,768]{2,1,0:T(8,128)(2,1)S(1)} %pad_maximum_fusion.1), channel_id=1, source_target_pairs={{0,192},{8,56},{16,208},{24,8},{32,224},{40,24},{48,240},{56,40},{... | collective-permute-start | bytes 2359304 | tf_op jit(solution)/shard_map/ppermute | solution.py:30
  108.9 13.3 %collective-permute-start.31 = (bf16[4,128,768]{2,1,0:T(8,128)(2,1)S(1)}, bf16[4,128,768]{2,1,0:T(8,128)(2,1)S(1)}, u32[]{:S(2)}, u32[]{:S(2)}) collective-permute-start(bf16[4,128,768]{2,1,0:T(8,128)(2,1)S(1)} %pad_maximum_fusion), channel_id=1, source_target_pairs={{0,64},{8,24},{16,80},{24,40},{32,96},{40,56},{48,112},{56,8},{64,... | collective-permute-start | bytes 2359304 | tf_op jit(solution)/shard_map/ppermute | solution.py:30
  109.0 6.5 %collective-permute-start.34 = (bf16[2,256,256]{2,1,0:T(8,128)(2,1)S(1)}, bf16[2,256,256]{2,1,0:T(8,128)(2,1)S(1)}, u32[]{:S(2)}, u32[]{:S(2)}) collective-permute-start(bf16[2,256,256]{2,1,0:T(8,128)(2,1)S(1)} %pad_maximum_fusion.3), channel_id=1, source_target_pairs={{0,1},{1,0},{2,3},{3,2},{4,5},{5,4},{6,7},{7,6},{8,9},{9,8},{10,11... | collective-permute-start | bytes 786440 | tf_op jit(solution)/shard_map/ppermute | solution.py:34
  124.3 7.3 %collective-permute-start.36 = (bf16[128,768]{1,0:T(8,128)(2,1)S(1)}, bf16[128,768]{1,0:T(8,128)(2,1)S(1)}, u32[]{:S(2)}, u32[]{:S(2)}) collective-permute-start(bf16[128,768]{1,0:T(8,128)(2,1)S(1)} %get-tuple-element.52), channel_id=1, source_target_pairs={{0,32},{8,136},{16,48},{24,152},{32,0},{40,168},{48,16},{56,184},{... | collective-permute-start | bytes 589832 | tf_op jit(solution)/shard_map/ppermute | solution.py:30
  125.8 7.8 %collective-permute-start.37 = (bf16[128,768]{1,0:T(8,128)(2,1)S(1)}, bf16[128,768]{1,0:T(8,128)(2,1)S(1)}, u32[]{:S(2)}, u32[]{:S(2)}) collective-permute-start(bf16[128,768]{1,0:T(8,128)(2,1)S(1)} %get-tuple-element.53), channel_id=1, source_target_pairs={{0,48},{8,200},{16,0},{24,216},{32,16},{40,232},{48,32},{56,248},{... | collective-permute-start | bytes 589832 | tf_op jit(solution)/shard_map/ppermute | solution.py:30
  135.2 8.7 %collective-permute-start.39 = (bf16[2,32,768]{2,1,0:T(8,128)(2,1)S(1)}, bf16[2,32,768]{2,1,0:T(8,128)(2,1)S(1)}, u32[]{:S(2)}, u32[]{:S(2)}) collective-permute-start(bf16[2,32,768]{2,1,0:T(8,128)(2,1)S(1)} %pad_maximum_fusion.5), channel_id=1, source_target_pairs={{0,7},{1,2},{2,1},{3,4},{4,3},{5,6},{6,5},{7,0},{8,15},{9,10},{10,... | collective-permute-start | bytes 294920 | tf_op jit(solution)/shard_map/ppermute | solution.py:38
  143.9 8.1 %collective-permute-start.40 = (bf16[2,32,768]{2,1,0:T(8,128)(2,1)S(1)}, bf16[2,32,768]{2,1,0:T(8,128)(2,1)S(1)}, u32[]{:S(2)}, u32[]{:S(2)}) collective-permute-start(bf16[2,32,768]{2,1,0:T(8,128)(2,1)S(1)} %add_convert_fusion.7), channel_id=1, source_target_pairs={{0,3},{1,6},{2,5},{3,0},{4,7},{5,2},{6,1},{7,4},{8,11},{9,14},{10,... | collective-permute-start | bytes 294920 | tf_op jit(solution)/shard_map/ppermute | solution.py:42
  (31 other events, 234.8 us)

commit v2 on v1

--- a/solution.py
+++ b/solution.py
@@ -69,14 +69,14 @@
     return pl.BlockSpec(memory_space=pltpu.VMEM)
 
 
-def call(kernel, args, n_smem, outs, scratch=(), grant=16, flops=0, nbytes=0, n_any=0):
+def call(kernel, args, n_smem, outs, scratch=(), grant=16, flops=0, nbytes=0, n_any=0, outs_any=False):
     return pl.pallas_call(
         kernel,
         out_shape=[jax.ShapeDtypeStruct(*out) for out in outs],
         in_specs=[smem()] * n_smem
         + [vmem()] * (len(args) - n_smem - n_any)
         + [pl.BlockSpec(memory_space=pl.ANY)] * n_any,
-        out_specs=[vmem()] * len(outs),
+        out_specs=[pl.BlockSpec(memory_space=pl.ANY) if outs_any else vmem()] * len(outs),
         scratch_shapes=list(scratch),
         compiler_params=pltpu.CompilerParams(vmem_limit_bytes=grant * MIB),
         cost_estimate=pl.CostEstimate(flops=flops, bytes_accessed=nbytes, transcendentals=0),
@@ -98,33 +98,33 @@
     return lam * bit.astype(F32) * (1.0 / math.sqrt(HEAD * 2 ** (level - 1) * BLOCK))
 
 
-def prepare_kernel(pos, w, w_own, w_core, sems):
+def prepare_kernel(pos, w, tok, cot, w_own, w_core, to_z, c_own, c_core, sems):
     core, kind = pos[2], pos[4]
     copies = []
-    for n, out in enumerate((w_core, w_own)):
-        group = ((1 - core if n == 0 else core) * 2 + kind) * 256
+
+    def columns(cs, zs):
+        group = ((core + cs) & 1) * 2 + ((kind + zs) & 1)
+        return pl.ds(pl.multiple_of(group * 256, 256), 256)
+
+    def bring(src, dst):
+        copies.append(pltpu.make_async_copy(src, dst, sems.at[len(copies)]))
+        copies[-1].start()
+
+    bring(tok, to_z.at[:, pl.ds(0, D)])
+    for cs, out in ((1, w_core), (0, w_own)):
         for third in range(3):
-            src = w.at[third, :, pl.ds(pl.multiple_of(group, 256), 256)]
-            dst = out.at[:, pl.ds(third * 256, 256)]
-            copies.append(pltpu.make_async_copy(src, dst, sems.at[n * 3 + third]))
-    for copy in copies:
-        copy.start()
+            bring(w.at[third, :, columns(cs, 0)], out.at[:, pl.ds(third * 256, 256)])
+    for cs, out in enumerate((c_own, c_core)):
+        bring(cot.at[:, columns(cs, 0)], out)
+        bring(cot.at[:, columns(cs, 1)], to_z.at[:, pl.ds(D + cs * 256, 256)])
     for copy in copies:
         copy.wait()
 
 
-def split_kernel(pos, cot, c_own, c_z):
-    core, kind = pos[2], pos[4]
-    for cs in range(2):
-        for zs, out in enumerate((c_own, c_z)):
-            group = ((core + cs) & 1) * 2 + ((kind + zs) & 1)
-            out[cs] = cot[:, pl.ds(pl.multiple_of(group * 256, 256), 256)]
-
-
 def project_kernel(pos, idx, table, *refs):
-    c_own, c_z, c_core = refs[4:7]
-    parts = (refs[7:9], refs[9:11], refs[13:15], refs[11:13])
-    qkv, cots, s1, x0, g1, m2, m3, m4, m5, w, toks, sems = refs[15:]
+    c_own, c_core = refs[4:6]
+    parts = (refs[6:8], refs[8:10], refs[12:14], refs[10:12])
+    qkv, cots, s1, x0, g1, m2, m3, m4, m5, w, toks, sems = refs[14:]
     y, x, core = pos[0], pos[1], pos[2]
     copies = []
 
@@ -141,8 +141,9 @@
                 start = (slot % 2) * 128 + cs * 64
                 bring(parts[dist][slot // 2].at[pl.ds(start, 64)], w.at[pl.ds(row, 64)])
     for blk in range(4):
-        bring(refs[blk], toks.at[blk])
-    for blk, src in enumerate((c_own.at[0], c_z.at[0], c_core.at[0], c_core.at[1])):
+        bring(refs[blk].at[:, pl.ds(0, D)], toks.at[blk])
+    near, across = refs[1].at[:, pl.ds(D, 256)], refs[3].at[:, pl.ds(D + 256, 256)]
+    for blk, src in enumerate((c_own, near, c_core, across)):
         bring(src, cots.at[blk])
     for copy in copies:
         copy.wait()
@@ -303,7 +304,7 @@
             attn_out[:, pl.ds(pl.multiple_of(group * 256, 256), 256)] = attns[cs][zs][...]
 
 
-def place_kernel(pos, mine, near, theirs, grad_w):
+def place_kernel(pos, mine, near, theirs, beyond, grad_w):
     core, kind = pos[2], pos[4]
     halves = (pos[5], pos[6])
     for cs in range(2):
@@ -311,7 +312,7 @@
             group = ((core + cs) & 1) * 2 + ((kind + zs) & 1)
             lane = pl.ds(pl.multiple_of(group * 256, 256), 256)
             for piece in range(2):
-                part = (mine, near)[piece] if zs == 0 else theirs.at[piece]
+                part = ((mine, near), (theirs, beyond))[zs][piece]
                 row = pl.ds(pl.multiple_of(((halves[zs] + piece) & 1) * 32, 32), 32)
                 for third in range(3):
                     grad_w[third, row, lane] = part[
@@ -339,15 +340,22 @@
     idx = jnp.concatenate([rows, swap(rows, "core", 2, 1)], axis=0)
     scalars = [pos, idx, weight_table]
 
-    w_own, w_core = call(
+    w_own, w_core, to_z, c_own, c_core = call(
         prepare_kernel,
-        [pos, jnp.transpose(w_qkv, (1, 0, 2))],
+        [pos, jnp.transpose(w_qkv, (1, 0, 2)), inputs, cotangent[0]],
         1,
-        [((64, COLS), BF), ((64, COLS), BF)],
-        scratch=[pltpu.SemaphoreType.DMA((6,))],
+        [
+            ((64, COLS), BF),
+            ((64, COLS), BF),
+            ((BLOCK, D + 512), BF),
+            ((BLOCK, 256), BF),
+            ((BLOCK, 256), BF),
+        ],
+        scratch=[pltpu.SemaphoreType.DMA((11,))],
         grant=48,
-        nbytes=MIB,
-        n_any=1,
+        nbytes=4 * MIB,
+        n_any=3,
+        outs_any=True,
     )
 
     chunk = jnp.concatenate([w_own, swap(w_core, "core", 2, 1)], axis=0)
@@ -357,27 +365,17 @@
     behind = [ring(part, 1, 3) for part in mine]
     far = [ring(behind[0], 1, 3), ring(ahead[1], 1, 1)]
 
-    tok01 = hold(swap(inputs, "dp", 8, 1), *far)
-    c_own, c_z = call(
-        split_kernel,
-        [pos, after(cotangent[0], chunk)],
-        1,
-        [((2, BLOCK, 256), BF), ((2, BLOCK, 256), BF)],
-        grant=48,
-        nbytes=MIB,
-    )
-    from_z = swap(c_z, "dp", 8, 1)
-    tok10 = swap(after(inputs, *mine), "core", 2, 1)
+    c_core = swap(c_core, "core", 2, 1)
+    tok10 = swap(inputs, "core", 2, 1)
+    tok01 = hold(swap(to_z, "dp", 8, 1), tok10, c_core, idx, *far, *ahead, *behind)
     tok11 = swap(tok01, "core", 2, 1)
-    to_core = jnp.stack([c_own[1], from_z[1]], axis=0)
-    c_core = swap(to_core, "core", 2, 1)
     toks = [inputs, tok01, tok10, tok11]
 
     square = (2, 2, HEAD, HEAD)
     wide = (4, 2, HEAD, HEAD)
     qkv, cots, s1, x0, g1, m2, m3, m4, m5 = call(
         project_kernel,
-        scalars + toks + [c_own, from_z, c_core] + mine + ahead + behind + far,
+        scalars + toks + [c_own, c_core] + mine + ahead + behind + far,
         3,
         [
             ((4, BLOCK, COLS), BF),
@@ -398,7 +396,7 @@
         grant=52,
         flops=2 * 1024 * D * COLS,
         nbytes=10 * MIB,
-        n_any=15,
+        n_any=14,
     )
 
     cx = [swap(x0, "x", 4, mask) for mask in (1, 2, 3)]
@@ -472,11 +470,12 @@
     mine = add(pair[:, :32], same_set_neighbour(pair[:, 32:]))
     mine = add(mine, same_set_far(mine))
     near = same_set_neighbour(mine)
-    theirs = swap(jnp.stack([mine, near], axis=0), "dp", 8, 1)
+    theirs = swap(mine, "dp", 8, 1)
+    beyond = swap(near, "dp", 8, 1)
 
     (grad_w,) = call(
         place_kernel,
-        [pos, mine, near, theirs],
+        [pos, mine, near, theirs, beyond],
         1,
         [((3, 64, 1024), F32)],
         grant=6,

time: 165 us -> 218 us (1.32)
  Pallas kernels: 28.7 us -> 62.4 us
  waiting for transfers between devices: 65.8 us -> 89.9 us
  starting transfers between devices: 60.5 us -> 54.7 us
    pallas_call x9 -> x8, Pallas kernels: 28.7 us -> 62.4 us  [call(): pl.pallas_call(kernel, out_shape=[jax.ShapeDtypeStruct(*out) for out in o...]
    ppermute x24, waiting for transfers between devices: 26.8 us -> 46.6 us  [swap(): return lax.ppermute(value, axis, [(i, i ^ mask) for i in range(size)])]
    ppermute x16, starting transfers between devices: 28.9 us -> 23.3 us  [ring(): return lax.ppermute(value, ('y', 'x', 'core'), pairs)]
    ppermute x16, waiting for transfers between devices: 26.9 us -> 31.2 us  [ring(): return lax.ppermute(value, ('y', 'x', 'core'), pairs)]
    unnamed x43 -> x51, local copies, waits for them, and re-layouts: 6.27 us -> 7.79 us
  transfers between devices with their start and end apart: 43 -> 43, of which waited for: 22 -> 26; matrix products, arithmetic and copies ran while one was open for 2% -> 1% of each run, Pallas kernels for 7% -> 5%
where the time goes in v2:
time: 218 us
  waiting for transfers between devices  89.9 us (41%)
  Pallas kernels  62.4 us (29%)
  starting transfers between devices  54.7 us (25%)
  local copies, waits for them, and re-layouts  8.11 us (4%)
    pallas_call x8, Pallas kernels, call(): pl.pallas_call(kernel, out_shape=[jax.ShapeDtypeStruct(*out) for out in o...  62.4 us
    ppermute x24, waiting for transfers between devices, swap(): return lax.ppermute(value, axis, [(i, i ^ mask) for i in range(size)])  46.6 us
    ppermute x16, waiting for transfers between devices, ring(): return lax.ppermute(value, ('y', 'x', 'core'), pairs)  31.2 us
    ppermute x16, starting transfers between devices, ring(): return lax.ppermute(value, ('y', 'x', 'core'), pairs)  23.3 us
    ppermute x24, starting transfers between devices, swap(): return lax.ppermute(value, axis, [(i, i ^ mask) for i in range(size)])  20.7 us
    ppermute x2, starting transfers between devices, same_set_neighbour(): lax.ppermute(value, 'dp', [(z, (z + 1 if z % 2 else z - 1) % 8) for z in...  8.7 us
    unnamed x51, local copies, waits for them, and re-layouts  7.79 us
    ppermute x1, waiting for transfers between devices, same_set_far(): lax.ppermute(value, 'dp', [(z, ((7 if SETS >> z & 1 else 3) - z) % 8) for...  6.07 us
  transfers between devices with their start and end apart: 43, of which 26 were waited for; matrix products, arithmetic and copies ran while one was open for 1% of the time, Pallas kernels for 5%

profile of v2, /device:TPU:6, one launch (start us, length us, event | category | flops | bytes accessed | tf_op | source)
XLA Modules:
  0.0 217.6 jit_solution(1054091558863204689)
XLA Ops:
  2.8 33.5 %shard_map.68 = (bf16[64,768]{1,0:T(8,128)(2,1)S(1)}, bf16[64,768]{1,0:T(8,128)(2,1)S(1)}, bf16[256,2560]{1,0:T(8,128)(2,1)}, bf16[256,256]{1,0:T(8,128)(2,1)S(1)}, bf16[256,256]{1,0:T(8,128)(2,1)S(1)}) custom-call(s32[7]{0:T(128)S(1)} %stack.43.pos, bf16[3,64,1024]{2,1,0:T(8,128)(2,1)S(1)} %bitcast.16, bf16[256,2048]{1,0:T(8,128)(2,1)} %bitcast.7.tok.refs_0_.t0, ...), custom_call_target="tpu_custom_call" | custom-call | bytes 4194304 | tf_op jit(solution)/shard_map/pallas_call | solution.py:73
  42.9 27.4 %collective-permute-done.3 = s32[1,12]{1,0:T(1,128)S(1)} collective-permute-done((s32[1,12]{1,0:T(1,128)S(1)}, s32[1,12]{1,0:T(1,128)S(1)}, u32[]{:S(2)}, u32[]{:S(2)}) %collective-permute-start.3) | collective-permute-done | bytes 80 | tf_op jit(solution)/shard_map/ppermute | solution.py:34
  70.3 2.5 %collective-permute-start.6 = (bf16[128,768]{1,0:T(8,128)(2,1)S(1)}, bf16[128,768]{1,0:T(8,128)(2,1)S(1)}, u32[]{:S(2)}, u32[]{:S(2)}) collective-permute-start(bf16[128,768]{1,0:T(8,128)(2,1)S(1)} %get-tuple-element.57), channel_id=1, source_target_pairs={{0,48},{8,200},{16,0},{24,216},{32,16},{40,232},{48,32},{56,248},{... | collective-permute-start | bytes 589832 | tf_op jit(solution)/shard_map/ppermute | solution.py:30
  73.6 3.5 %collective-permute-done.6 = bf16[128,768]{1,0:T(8,128)(2,1)S(1)} collective-permute-done((bf16[128,768]{1,0:T(8,128)(2,1)S(1)}, bf16[128,768]{1,0:T(8,128)(2,1)S(1)}, u32[]{:S(2)}, u32[]{:S(2)}) %collective-permute-start.6) | collective-permute-done | bytes 196640 | tf_op jit(solution)/shard_map/ppermute | solution.py:30
  80.7 2.7 %collective-permute-start.11 = (bf16[256,768]{1,0:T(8,128)(2,1)S(1)}, bf16[256,768]{1,0:T(8,128)(2,1)S(1)}, u32[]{:S(2)}, u32[]{:S(2)}) collective-permute-start(bf16[256,768]{1,0:T(8,128)(2,1)S(1)} %constant_dynamic-update-slice_fusion.5.refs_7_), channel_id=1, source_target_pairs={{0,192},{8,56},{16,208},{24,8},{32,224},{40,24},{48,240},{56,40},{... | collective-permute-start | bytes 1179656 | tf_op jit(solution)/shard_map/ppermute | solution.py:30
  83.4 2.9 %collective-permute-done.13.refs_6_.refs_8_ = bf16[256,768]{1,0:T(8,128)(2,1)S(1)} collective-permute-done((bf16[256,768]{1,0:T(8,128)(2,1)S(1)}, bf16[256,768]{1,0:T(8,128)(2,1)S(1)}, u32[]{:S(2)}, u32[]{:S(2)}) %collective-permute-start.13) | collective-permute-done | bytes 393248 | tf_op jit(solution)/shard_map/ppermute | solution.py:30
  90.5 2.7 %collective-permute-start.12 = (bf16[256,768]{1,0:T(8,128)(2,1)S(1)}, bf16[256,768]{1,0:T(8,128)(2,1)S(1)}, u32[]{:S(2)}, u32[]{:S(2)}) collective-permute-start(bf16[256,768]{1,0:T(8,128)(2,1)S(1)} %collective-permute-done.11.refs_7_.refs_9_), channel_id=1, source_target_pairs={{0,192},{8,56},{16,208},{24,8},{32,224},{40,24},{48,240},{56,40},{... | collective-permute-start | bytes 1179656 | tf_op jit(solution)/shard_map/ppermute | solution.py:30
  95.3 4.2 %collective-permute-done.8.refs_4_.refs_12_ = bf16[256,768]{1,0:T(8,128)(2,1)S(1)} collective-permute-done((bf16[256,768]{1,0:T(8,128)(2,1)S(1)}, bf16[256,768]{1,0:T(8,128)(2,1)S(1)}, u32[]{:S(2)}, u32[]{:S(2)}) %collective-permute-start.8) | collective-permute-done | bytes 393248 | tf_op jit(solution)/shard_map/ppermute | solution.py:30
  102.3 3.2 %collective-permute-done.15.refs_3_.t3 = bf16[256,2560]{1,0:T(8,128)(2,1)S(1)} collective-permute-done((bf16[256,2560]{1,0:T(8,128)(2,1)}, bf16[256,2560]{1,0:T(8,128)(2,1)S(1)}, u32[]{:S(2)}, u32[]{:S(2)}) %collective-permute-start.15) | collective-permute-done | bytes 1310752 | tf_op jit(solution)/shard_map/ppermute | solution.py:34
  107.4 11.0 %shard_map.70 = (bf16[4,256,768]{2,1,0:T(8,128)(2,1)}, bf16[4,256,256]{2,1,0:T(8,128)(2,1)}, bf16[4,2,128,128]{3,2,1,0:T(8,128)(2,1)S(1)}, bf16[2,2,128,128]{3,2...) custom-call(s32[7]{0:T(128)S(1)} %stack.43.pos, ...), custom_call_target="tpu_custom_call" | custom-call | flops 3221225472 | bytes 10485760 | tf_op jit(solution)/shard_map/pallas_call | solution.py:73
  122.6 2.7 %collective-permute-start.18 = (bf16[2,2,128,128]{3,2,1,0:T(8,128)(2,1)S(1)}, bf16[2,2,128,128]{3,2,1,0:T(8,128)(2,1)S(1)}, u32[]{:S(2)}, u32[]{:S(2)}) collective-permute-start(bf16[2,2,128,128]{3,2,1,0:T(8,128)(2,1)S(1)} %get-tuple-element.36), channel_id=1, source_target_pairs={{0,48},{16,32},{32,16},{48,0},{1,49},{17,33},{33,17},{49,1},{2,50}... | collective-permute-start | bytes 393224 | tf_op jit(solution)/shard_map/ppermute | solution.py:34
  128.4 3.3 %collective-permute-start.27 = (bf16[2,2,128,128]{3,2,1,0:T(8,128)(2,1)S(1)}, bf16[2,2,128,128]{3,2,1,0:T(8,128)(2,1)S(1)}, u32[]{:S(2)}, u32[]{:S(2)}) collective-permute-start(bf16[2,2,128,128]{3,2,1,0:T(8,128)(2,1)S(1)} %get-tuple-element.52), channel_id=1, source_target_pairs={{0,48},{16,32},{32,16},{48,0},{1,49},{17,33},{33,17},{49,1},{2,50}... | collective-permute-start | bytes 393224 | tf_op jit(solution)/shard_map/ppermute | solution.py:34
  132.9 2.4 %collective-permute-start.21 = (bf16[2,2,128,128]{3,2,1,0:T(8,128)(2,1)S(1)}, bf16[2,2,128,128]{3,2,1,0:T(8,128)(2,1)S(1)}, u32[]{:S(2)}, u32[]{:S(2)}) collective-permute-start(bf16[2,2,128,128]{3,2,1,0:T(8,128)(2,1)S(1)} %add_convert_fusion.5), channel_id=1, source_target_pairs={{0,192},{64,128},{128,64},{192,0},{1,193},{65,129},{129,65},{193,1... | collective-permute-start | bytes 393224 | tf_op jit(solution)/shard_map/ppermute | solution.py:34
  135.4 2.8 %collective-permute-done.25.refs_16_ = bf16[2,2,128,128]{3,2,1,0:T(8,128)(2,1)S(1)} collective-permute-done((bf16[2,2,128,128]{3,2,1,0:T(8,128)(2,1)S(1)}, bf16[2,2,128,128]{3,2,1,0:T(8,128)(2,1)S(1)}, u32[]{:S(2)}, u32[]{:S(2)}) %collective-permute-start.25) | collective-permute-done | bytes 131104 | tf_op jit(solution)/shard_map/ppermute | solution.py:34
  139.2 5.1 %shard_map.71.refs_6_ = f32[4,256,1024]{2,1,0:T(8,128)S(1)} custom-call(s32[7]{0:T(128)S(1)} %stack.43.pos, s32[4,12]{1,0:T(4,128)S(1)} %copy-done.14, f32[16,8]{1,0:T(8,128)S(1)} %copy.10.table, bf16[4,256,768]{2,1,0:T(8,128)(2,1)S(1)} %copy-done.6, bf16[4,256,256]{2,1,0:T(8,128)(2,1)S(1)} %copy-done.7), custom_call_target="tpu_custom_call" | custom-call | flops 805306368 | bytes 8388608 | tf_op jit(solution)/shard_map/pallas_call | solution.py:73
  144.5 3.9 %shard_map.72 = (bf16[4,256,256]{2,1,0:T(8,128)(2,1)S(1)}, bf16[4,256,768]{2,1,0:T(8,128)(2,1)S(1)}, bf16[2,128,768]{2,1,0:T(8,128)(2,1)S(1)}, bf16[2,128,768]{2,1,0:T(8,128)(2,1)S(1)}) custom-call(s32[7]{0:T(128)S(1)} %stack.43.pos, s32[4,12]{1,0:T(4,128)S(1)} %copy-done.14, f32[16,8]{1,0:T(8,128)S(1)} %copy.10.table, ...), custom_call_target="tpu_custom_call" | custom-call | flops 1610612736 | bytes 12582912 | tf_op jit(solution)/shard_map/pallas_call | solution.py:73
  148.5 2.1 collective-permute-start.31
  150.9 3.3 %shard_map.74 = (bf16[4,128,768]{2,1,0:T(8,128)(2,1)S(1)}, bf16[4,128,768]{2,1,0:T(8,128)(2,1)S(1)}) custom-call(s32[7]{0:T(128)S(1)} %stack.43.pos, bf16[256,2048]{1,0:T(8,128)(2,1)} %bitcast.7.tok.refs_0_.t0, bf16[256,2560]{1,0:T(8,128)(2,1)S(1)} %copy-done.1, bf16[256,2048]{1,0:T(8,128)(2,1)S(1)} %copy-done.3, bf16[256,2560]{1,0:T(8,128)(2,1)S(1)} %copy-done.5, ...), custom_call_target="tpu_custom_call" | custom-call | flops 1610612736 | bytes 9437184 | tf_op jit(solution)/shard_map/pallas_call | solution.py:73
  154.3 2.1 collective-permute-done.31
  156.5 3.3 %collective-permute-start.32 = (bf16[4,128,768]{2,1,0:T(8,128)(2,1)S(1)}, bf16[4,128,768]{2,1,0:T(8,128)(2,1)S(1)}, u32[]{:S(2)}, u32[]{:S(2)}) collective-permute-start(bf16[4,128,768]{2,1,0:T(8,128)(2,1)S(1)} %pad_maximum_fusion.1), channel_id=1, source_target_pairs={{0,192},{8,56},{16,208},{24,8},{32,224},{40,24},{48,240},{56,40},{... | collective-permute-start | bytes 2359304 | tf_op jit(solution)/shard_map/ppermute | solution.py:30
  162.0 2.5 %shard_map.73.own = bf16[4,128,768]{2,1,0:T(8,128)(2,1)S(1)} custom-call(s32[7]{0:T(128)S(1)} %stack.43.pos, bf16[256,2048]{1,0:T(8,128)(2,1)} %bitcast.7.tok.refs_0_.t0, bf16[256,2560]{1,0:T(8,128)(2,1)S(1)} %copy-done.1, bf16[256,2048]{1,0:T(8,128)(2,1)S(1)} %copy-done.3, bf16[256,2560]{1,0:T(8,128)(2,1)S(1)} %copy-done.5, ...), custom_call_target="tpu_custom_call" | custom-call | flops 402653184 | bytes 9437184 | tf_op jit(solution)/shard_map/pallas_call | solution.py:73
  164.5 4.3 %collective-permute-done.33.from_z = bf16[2,256,256]{2,1,0:T(8,128)(2,1)S(1)} collective-permute-done((bf16[2,256,256]{2,1,0:T(8,128)(2,1)S(1)}, bf16[2,256,256]{2,1,0:T(8,128)(2,1)S(1)}, u32[]{:S(2)}, u32[]{:S(2)}) %collective-permute-start.33) | collective-permute-done | bytes 262176 | tf_op jit(solution)/shard_map/ppermute | solution.py:34
  169.3 3.9 %collective-permute-done.30.r1 = bf16[4,128,768]{2,1,0:T(8,128)(2,1)S(1)} collective-permute-done((bf16[4,128,768]{2,1,0:T(8,128)(2,1)S(1)}, bf16[4,128,768]{2,1,0:T(8,128)(2,1)S(1)}, u32[]{:S(2)}, u32[]{:S(2)}) %collective-permute-start.30) | collective-permute-done | bytes 786464 | tf_op jit(solution)/shard_map/ppermute | solution.py:30
  174.9 3.1 %collective-permute-start.34 = (bf16[128,768]{1,0:T(8,128)(2,1)S(1)}, bf16[128,768]{1,0:T(8,128)(2,1)S(1)}, u32[]{:S(2)}, u32[]{:S(2)}) collective-permute-start(bf16[128,768]{1,0:T(8,128)(2,1)S(1)} %get-tuple-element.49), channel_id=1, source_target_pairs={{0,16},{8,72},{16,32},{24,88},{32,48},{40,104},{48,0},{56,120},{64... | collective-permute-start | bytes 589832 | tf_op jit(solution)/shard_map/ppermute | solution.py:30
  178.9 4.4 %collective-permute-done.34 = bf16[128,768]{1,0:T(8,128)(2,1)S(1)} collective-permute-done((bf16[128,768]{1,0:T(8,128)(2,1)S(1)}, bf16[128,768]{1,0:T(8,128)(2,1)S(1)}, u32[]{:S(2)}, u32[]{:S(2)}) %collective-permute-start.34) | collective-permute-done | bytes 196640 | tf_op jit(solution)/shard_map/ppermute | solution.py:30
  188.6 5.8 %collective-permute-start.38 = (bf16[2,32,768]{2,1,0:T(8,128)(2,1)S(1)}, bf16[2,32,768]{2,1,0:T(8,128)(2,1)S(1)}, u32[]{:S(2)}, u32[]{:S(2)}) collective-permute-start(bf16[2,32,768]{2,1,0:T(8,128)(2,1)S(1)} %pad_maximum_fusion.3), channel_id=1, source_target_pairs={{0,7},{1,2},{2,1},{3,4},{4,3},{5,6},{6,5},{7,0},{8,15},{9,10},{10,... | collective-permute-start | bytes 294920 | tf_op jit(solution)/shard_map/ppermute | solution.py:38
  194.4 3.1 %collective-permute-done.38 = bf16[2,32,768]{2,1,0:T(8,128)(2,1)S(1)} collective-permute-done((bf16[2,32,768]{2,1,0:T(8,128)(2,1)S(1)}, bf16[2,32,768]{2,1,0:T(8,128)(2,1)S(1)}, u32[]{:S(2)}, u32[]{:S(2)}) %collective-permute-start.38) | collective-permute-done | bytes 98336 | tf_op jit(solution)/shard_map/ppermute | solution.py:38
  199.4 6.1 %collective-permute-done.39 = bf16[2,32,768]{2,1,0:T(8,128)(2,1)S(1)} collective-permute-done((bf16[2,32,768]{2,1,0:T(8,128)(2,1)S(1)}, bf16[2,32,768]{2,1,0:T(8,128)(2,1)S(1)}, u32[]{:S(2)}, u32[]{:S(2)}) %collective-permute-start.39) | collective-permute-done | bytes 98336 | tf_op jit(solution)/shard_map/ppermute | solution.py:42
  205.6 2.9 %collective-permute-start.40 = (bf16[2,32,768]{2,1,0:T(8,128)(2,1)S(1)}, bf16[2,32,768]{2,1,0:T(8,128)(2,1)S(1)}, u32[]{:S(2)}, u32[]{:S(2)}) collective-permute-start(bf16[2,32,768]{2,1,0:T(8,128)(2,1)S(1)} %add_convert_fusion.6.mine), channel_id=1, source_target_pairs={{0,7},{1,2},{2,1},{3,4},{4,3},{5,6},{6,5},{7,0},{8,15},{9,10},{10,... | collective-permute-start | bytes 294920 | tf_op jit(solution)/shard_map/ppermute | solution.py:38
  208.5 3.0 %collective-permute-done.40.near = bf16[2,32,768]{2,1,0:T(8,128)(2,1)S(1)} collective-permute-done((bf16[2,32,768]{2,1,0:T(8,128)(2,1)S(1)}, bf16[2,32,768]{2,1,0:T(8,128)(2,1)S(1)}, u32[]{:S(2)}, u32[]{:S(2)}) %collective-permute-start.40) | collective-permute-done | bytes 98336 | tf_op jit(solution)/shard_map/ppermute | solution.py:38
  211.5 2.5 %collective-permute-done.41.theirs = bf16[2,32,768]{2,1,0:T(8,128)(2,1)S(1)} collective-permute-done((bf16[2,32,768]{2,1,0:T(8,128)(2,1)S(1)}, bf16[2,32,768]{2,1,0:T(8,128)(2,1)S(1)}, u32[]{:S(2)}, u32[]{:S(2)}) %collective-permute-start.41) | collective-permute-done | bytes 98336 | tf_op jit(solution)/shard_map/ppermute | solution.py:34
  214.0 2.1 collective-permute-done.42.beyond
  (138 shorter events, 48.0 us)
Async XLA Ops:
  37.7 35.1 %collective-permute-start.9 = (bf16[128,768]{1,0:T(8,128)(2,1)S(1)}, bf16[128,768]{1,0:T(8,128)(2,1)S(1)}, u32[]{:S(2)}, u32[]{:S(2)}) collective-permute-start(bf16[128,768]{1,0:T(8,128)(2,1)S(1)} %get-tuple-element.57), channel_id=1, source_target_pairs={{0,32},{8,136},{16,48},{24,152},{32,0},{40,168},{48,16},{56,184},{... | collective-permute-start | bytes 589832 | tf_op jit(solution)/shard_map/ppermute | solution.py:30
  39.2 61.9 %collective-permute-start = (bf16[256,2560]{1,0:T(8,128)(2,1)}, bf16[256,2560]{1,0:T(8,128)(2,1)S(1)}, u32[]{:S(2)}, u32[]{:S(2)}) collective-permute-start(bf16[256,2560]{1,0:T(8,128)(2,1)} %get-tuple-element.27), channel_id=1, source_target_pairs={{0,1},{1,0},{2,3},{3,2},{4,5},{5,4},{6,7},{7,6},{8,9},{9,8},{10,11... | collective-permute-start | bytes 3932168 | tf_op jit(solution)/shard_map/ppermute | solution.py:34
  41.1 54.2 %collective-permute-start.1 = (bf16[256,2048]{1,0:T(8,128)(2,1)}, bf16[256,2048]{1,0:T(8,128)(2,1)S(1)}, u32[]{:S(2)}, u32[]{:S(2)}) collective-permute-start(bf16[256,2048]{1,0:T(8,128)(2,1)} %bitcast.7.tok.refs_0_.t0), channel_id=1, source_target_pairs={{0,8},{8,0},{1,9},{9,1},{2,10},{10,2},{3,11},{11,3},{4,12},{12,4},... | collective-permute-start | bytes 3145736 | tf_op jit(solution)/shard_map/ppermute | solution.py:34
  42.6 27.7 %collective-permute-start.3 = (s32[1,12]{1,0:T(1,128)S(1)}, s32[1,12]{1,0:T(1,128)S(1)}, u32[]{:S(2)}, u32[]{:S(2)}) collective-permute-start(s32[1,12]{1,0:T(1,128)S(1)} %reshape.7), channel_id=1, source_target_pairs={{0,1},{1,0},{2,3},{3,2},{4,5},{5,4},{6,7},{7,6},{8,9},{9,8},{10,11... | collective-permute-start | bytes 152 | tf_op jit(solution)/shard_map/ppermute | solution.py:34
  42.9 37.8 %collective-permute-start.2 = (bf16[256,256]{1,0:T(8,128)(2,1)S(1)}, bf16[256,256]{1,0:T(8,128)(2,1)S(1)}, u32[]{:S(2)}, u32[]{:S(2)}) collective-permute-start(bf16[256,256]{1,0:T(8,128)(2,1)S(1)} %get-tuple-element.28), channel_id=1, source_target_pairs={{0,8},{8,0},{1,9},{9,1},{2,10},{10,2},{3,11},{11,3},{4,12},{12,4},... | collective-permute-start | bytes 393224 | tf_op jit(solution)/shard_map/ppermute | solution.py:34
  70.3 6.9 %collective-permute-start.6 = (bf16[128,768]{1,0:T(8,128)(2,1)S(1)}, bf16[128,768]{1,0:T(8,128)(2,1)S(1)}, u32[]{:S(2)}, u32[]{:S(2)}) collective-permute-start(bf16[128,768]{1,0:T(8,128)(2,1)S(1)} %get-tuple-element.57), channel_id=1, source_target_pairs={{0,48},{8,200},{16,0},{24,216},{32,16},{40,232},{48,32},{56,248},{... | collective-permute-start | bytes 589832 | tf_op jit(solution)/shard_map/ppermute | solution.py:30
  78.5 7.8 %collective-permute-start.13 = (bf16[256,768]{1,0:T(8,128)(2,1)S(1)}, bf16[256,768]{1,0:T(8,128)(2,1)S(1)}, u32[]{:S(2)}, u32[]{:S(2)}) collective-permute-start(bf16[256,768]{1,0:T(8,128)(2,1)S(1)} %constant_dynamic-update-slice_fusion.2.refs_6_), channel_id=1, source_target_pairs={{0,192},{8,56},{16,208},{24,8},{32,224},{40,24},{48,240},{56,40},{... | collective-permute-start | bytes 1179656 | tf_op jit(solution)/shard_map/ppermute | solution.py:30
  80.1 9.1 %collective-permute-start.7 = (bf16[256,768]{1,0:T(8,128)(2,1)S(1)}, bf16[256,768]{1,0:T(8,128)(2,1)S(1)}, u32[]{:S(2)}, u32[]{:S(2)}) collective-permute-start(bf16[256,768]{1,0:T(8,128)(2,1)S(1)} %constant_dynamic-update-slice_fusion.2.refs_6_), channel_id=1, source_target_pairs={{0,64},{8,24},{16,80},{24,40},{32,96},{40,56},{48,112},{56,8},{64,... | collective-permute-start | bytes 1179656 | tf_op jit(solution)/shard_map/ppermute | solution.py:30
  80.7 9.8 %collective-permute-start.11 = (bf16[256,768]{1,0:T(8,128)(2,1)S(1)}, bf16[256,768]{1,0:T(8,128)(2,1)S(1)}, u32[]{:S(2)}, u32[]{:S(2)}) collective-permute-start(bf16[256,768]{1,0:T(8,128)(2,1)S(1)} %constant_dynamic-update-slice_fusion.5.refs_7_), channel_id=1, source_target_pairs={{0,192},{8,56},{16,208},{24,8},{32,224},{40,24},{48,240},{56,40},{... | collective-permute-start | bytes 1179656 | tf_op jit(solution)/shard_map/ppermute | solution.py:30
  86.3 9.0 %collective-permute-start.14 = (bf16[256,768]{1,0:T(8,128)(2,1)S(1)}, bf16[256,768]{1,0:T(8,128)(2,1)S(1)}, u32[]{:S(2)}, u32[]{:S(2)}) collective-permute-start(bf16[256,768]{1,0:T(8,128)(2,1)S(1)} %constant_dynamic-update-slice_fusion.5.refs_7_), channel_id=1, source_target_pairs={{0,64},{8,24},{16,80},{24,40},{32,96},{40,56},{48,112},{56,8},{64,... | collective-permute-start | bytes 1179656 | tf_op jit(solution)/shard_map/ppermute | solution.py:30
  89.1 10.4 %collective-permute-start.8 = (bf16[256,768]{1,0:T(8,128)(2,1)S(1)}, bf16[256,768]{1,0:T(8,128)(2,1)S(1)}, u32[]{:S(2)}, u32[]{:S(2)}) collective-permute-start(bf16[256,768]{1,0:T(8,128)(2,1)S(1)} %collective-permute-done.7.refs_8_.refs_10_), channel_id=1, source_target_pairs={{0,64},{8,24},{16,80},{24,40},{32,96},{40,56},{48,112},{56,8},{64,... | collective-permute-start | bytes 1179656 | tf_op jit(solution)/shard_map/ppermute | solution.py:30
  90.5 9.0 %collective-permute-start.12 = (bf16[256,768]{1,0:T(8,128)(2,1)S(1)}, bf16[256,768]{1,0:T(8,128)(2,1)S(1)}, u32[]{:S(2)}, u32[]{:S(2)}) collective-permute-start(bf16[256,768]{1,0:T(8,128)(2,1)S(1)} %collective-permute-done.11.refs_7_.refs_9_), channel_id=1, source_target_pairs={{0,192},{8,56},{16,208},{24,8},{32,224},{40,24},{48,240},{56,40},{... | collective-permute-start | bytes 1179656 | tf_op jit(solution)/shard_map/ppermute | solution.py:30
  118.4 6.9 %collective-permute-start.22 = (bf16[2,2,128,128]{3,2,1,0:T(8,128)(2,1)S(1)}, bf16[2,2,128,128]{3,2,1,0:T(8,128)(2,1)S(1)}, u32[]{:S(2)}, u32[]{:S(2)}) collective-permute-start(bf16[2,2,128,128]{3,2,1,0:T(8,128)(2,1)S(1)} %get-tuple-element.37), channel_id=1, source_target_pairs={{0,64},{64,0},{128,192},{192,128},{1,65},{65,1},{129,193},{193,129... | collective-permute-start | bytes 393224 | tf_op jit(solution)/shard_map/ppermute | solution.py:34
  118.5 8.2 %collective-permute-start.24 = (bf16[2,2,128,128]{3,2,1,0:T(8,128)(2,1)S(1)}, bf16[2,2,128,128]{3,2,1,0:T(8,128)(2,1)S(1)}, u32[]{:S(2)}, u32[]{:S(2)}) collective-permute-start(bf16[2,2,128,128]{3,2,1,0:T(8,128)(2,1)S(1)} %get-tuple-element.38), channel_id=1, source_target_pairs={{0,192},{64,128},{128,64},{192,0},{1,193},{65,129},{129,65},{193,1... | collective-permute-start | bytes 393224 | tf_op jit(solution)/shard_map/ppermute | solution.py:34
  120.6 7.7 %collective-permute-start.23 = (bf16[2,2,128,128]{3,2,1,0:T(8,128)(2,1)S(1)}, bf16[2,2,128,128]{3,2,1,0:T(8,128)(2,1)S(1)}, u32[]{:S(2)}, u32[]{:S(2)}) collective-permute-start(bf16[2,2,128,128]{3,2,1,0:T(8,128)(2,1)S(1)} %get-tuple-element.38), channel_id=1, source_target_pairs={{0,128},{64,192},{128,0},{192,64},{1,129},{65,193},{129,1},{193,65... | collective-permute-start | bytes 393224 | tf_op jit(solution)/shard_map/ppermute | solution.py:34
  122.6 9.1 %collective-permute-start.18 = (bf16[2,2,128,128]{3,2,1,0:T(8,128)(2,1)S(1)}, bf16[2,2,128,128]{3,2,1,0:T(8,128)(2,1)S(1)}, u32[]{:S(2)}, u32[]{:S(2)}) collective-permute-start(bf16[2,2,128,128]{3,2,1,0:T(8,128)(2,1)S(1)} %get-tuple-element.36), channel_id=1, source_target_pairs={{0,48},{16,32},{32,16},{48,0},{1,49},{17,33},{33,17},{49,1},{2,50}... | collective-permute-start | bytes 393224 | tf_op jit(solution)/shard_map/ppermute | solution.py:34
  125.3 7.5 %collective-permute-start.17 = (bf16[2,2,128,128]{3,2,1,0:T(8,128)(2,1)S(1)}, bf16[2,2,128,128]{3,2,1,0:T(8,128)(2,1)S(1)}, u32[]{:S(2)}, u32[]{:S(2)}) collective-permute-start(bf16[2,2,128,128]{3,2,1,0:T(8,128)(2,1)S(1)} %get-tuple-element.36), channel_id=1, source_target_pairs={{0,32},{16,48},{32,0},{48,16},{1,33},{17,49},{33,1},{49,17},{2,34}... | collective-permute-start | bytes 393224 | tf_op jit(solution)/shard_map/ppermute | solution.py:34
  125.3 7.5 %collective-permute-start.16 = (bf16[2,2,128,128]{3,2,1,0:T(8,128)(2,1)S(1)}, bf16[2,2,128,128]{3,2,1,0:T(8,128)(2,1)S(1)}, u32[]{:S(2)}, u32[]{:S(2)}) collective-permute-start(bf16[2,2,128,128]{3,2,1,0:T(8,128)(2,1)S(1)} %get-tuple-element.36), channel_id=1, source_target_pairs={{0,16},{16,0},{32,48},{48,32},{1,17},{17,1},{33,49},{49,33},{2,18}... | collective-permute-start | bytes 393224 | tf_op jit(solution)/shard_map/ppermute | solution.py:34
  128.4 16.0 %collective-permute-start.27 = (bf16[2,2,128,128]{3,2,1,0:T(8,128)(2,1)S(1)}, bf16[2,2,128,128]{3,2,1,0:T(8,128)(2,1)S(1)}, u32[]{:S(2)}, u32[]{:S(2)}) collective-permute-start(bf16[2,2,128,128]{3,2,1,0:T(8,128)(2,1)S(1)} %get-tuple-element.52), channel_id=1, source_target_pairs={{0,48},{16,32},{32,16},{48,0},{1,49},{17,33},{33,17},{49,1},{2,50}... | collective-permute-start | bytes 393224 | tf_op jit(solution)/shard_map/ppermute | solution.py:34
  131.7 12.7 %collective-permute-start.26 = (bf16[2,2,128,128]{3,2,1,0:T(8,128)(2,1)S(1)}, bf16[2,2,128,128]{3,2,1,0:T(8,128)(2,1)S(1)}, u32[]{:S(2)}, u32[]{:S(2)}) collective-permute-start(bf16[2,2,128,128]{3,2,1,0:T(8,128)(2,1)S(1)} %get-tuple-element.52), channel_id=1, source_target_pairs={{0,32},{16,48},{32,0},{48,16},{1,33},{17,49},{33,1},{49,17},{2,34}... | collective-permute-start | bytes 393224 | tf_op jit(solution)/shard_map/ppermute | solution.py:34
  132.9 11.4 %collective-permute-start.21 = (bf16[2,2,128,128]{3,2,1,0:T(8,128)(2,1)S(1)}, bf16[2,2,128,128]{3,2,1,0:T(8,128)(2,1)S(1)}, u32[]{:S(2)}, u32[]{:S(2)}) collective-permute-start(bf16[2,2,128,128]{3,2,1,0:T(8,128)(2,1)S(1)} %add_convert_fusion.5), channel_id=1, source_target_pairs={{0,192},{64,128},{128,64},{192,0},{1,193},{65,129},{129,65},{193,1... | collective-permute-start | bytes 393224 | tf_op jit(solution)/shard_map/ppermute | solution.py:34
  135.4 9.0 %collective-permute-start.20 = (bf16[2,2,128,128]{3,2,1,0:T(8,128)(2,1)S(1)}, bf16[2,2,128,128]{3,2,1,0:T(8,128)(2,1)S(1)}, u32[]{:S(2)}, u32[]{:S(2)}) collective-permute-start(bf16[2,2,128,128]{3,2,1,0:T(8,128)(2,1)S(1)} %add_convert_fusion.5), channel_id=1, source_target_pairs={{0,128},{64,192},{128,0},{192,64},{1,129},{65,193},{129,1},{193,65... | collective-permute-start | bytes 393224 | tf_op jit(solution)/shard_map/ppermute | solution.py:34
  148.5 7.9 %collective-permute-start.31 = (bf16[2,128,768]{2,1,0:T(8,128)(2,1)S(1)}, bf16[2,128,768]{2,1,0:T(8,128)(2,1)S(1)}, u32[]{:S(2)}, u32[]{:S(2)}) collective-permute-start(bf16[2,128,768]{2,1,0:T(8,128)(2,1)S(1)} %get-tuple-element.46), channel_id=1, source_target_pairs={{0,192},{8,56},{16,208},{24,8},{32,224},{40,24},{48,240},{56,40},{... | collective-permute-start | bytes 1179656 | tf_op jit(solution)/shard_map/ppermute | solution.py:30
  150.6 9.2 %collective-permute-start.29 = (bf16[2,128,768]{2,1,0:T(8,128)(2,1)S(1)}, bf16[2,128,768]{2,1,0:T(8,128)(2,1)S(1)}, u32[]{:S(2)}, u32[]{:S(2)}) collective-permute-start(bf16[2,128,768]{2,1,0:T(8,128)(2,1)S(1)} %get-tuple-element.44), channel_id=1, source_target_pairs={{0,64},{8,24},{16,80},{24,40},{32,96},{40,56},{48,112},{56,8},{64,... | collective-permute-start | bytes 1179656 | tf_op jit(solution)/shard_map/ppermute | solution.py:30
  156.5 12.8 %collective-permute-start.32 = (bf16[4,128,768]{2,1,0:T(8,128)(2,1)S(1)}, bf16[4,128,768]{2,1,0:T(8,128)(2,1)S(1)}, u32[]{:S(2)}, u32[]{:S(2)}) collective-permute-start(bf16[4,128,768]{2,1,0:T(8,128)(2,1)S(1)} %pad_maximum_fusion.1), channel_id=1, source_target_pairs={{0,192},{8,56},{16,208},{24,8},{32,224},{40,24},{48,240},{56,40},{... | collective-permute-start | bytes 2359304 | tf_op jit(solution)/shard_map/ppermute | solution.py:30
  160.0 13.3 %collective-permute-start.30 = (bf16[4,128,768]{2,1,0:T(8,128)(2,1)S(1)}, bf16[4,128,768]{2,1,0:T(8,128)(2,1)S(1)}, u32[]{:S(2)}, u32[]{:S(2)}) collective-permute-start(bf16[4,128,768]{2,1,0:T(8,128)(2,1)S(1)} %pad_maximum_fusion), channel_id=1, source_target_pairs={{0,64},{8,24},{16,80},{24,40},{32,96},{40,56},{48,112},{56,8},{64,... | collective-permute-start | bytes 2359304 | tf_op jit(solution)/shard_map/ppermute | solution.py:30
  160.2 8.7 %collective-permute-start.33 = (bf16[2,256,256]{2,1,0:T(8,128)(2,1)S(1)}, bf16[2,256,256]{2,1,0:T(8,128)(2,1)S(1)}, u32[]{:S(2)}, u32[]{:S(2)}) collective-permute-start(bf16[2,256,256]{2,1,0:T(8,128)(2,1)S(1)} %pad_maximum_fusion.2), channel_id=1, source_target_pairs={{0,1},{1,0},{2,3},{3,2},{4,5},{5,4},{6,7},{7,6},{8,9},{9,8},{10,11... | collective-permute-start | bytes 786440 | tf_op jit(solution)/shard_map/ppermute | solution.py:34
  174.9 8.4 %collective-permute-start.34 = (bf16[128,768]{1,0:T(8,128)(2,1)S(1)}, bf16[128,768]{1,0:T(8,128)(2,1)S(1)}, u32[]{:S(2)}, u32[]{:S(2)}) collective-permute-start(bf16[128,768]{1,0:T(8,128)(2,1)S(1)} %get-tuple-element.49), channel_id=1, source_target_pairs={{0,16},{8,72},{16,32},{24,88},{32,48},{40,104},{48,0},{56,120},{64... | collective-permute-start | bytes 589832 | tf_op jit(solution)/shard_map/ppermute | solution.py:30
  178.0 7.3 %collective-permute-start.35 = (bf16[128,768]{1,0:T(8,128)(2,1)S(1)}, bf16[128,768]{1,0:T(8,128)(2,1)S(1)}, u32[]{:S(2)}, u32[]{:S(2)}) collective-permute-start(bf16[128,768]{1,0:T(8,128)(2,1)S(1)} %get-tuple-element.50), channel_id=1, source_target_pairs={{0,32},{8,136},{16,48},{24,152},{32,0},{40,168},{48,16},{56,184},{... | collective-permute-start | bytes 589832 | tf_op jit(solution)/shard_map/ppermute | solution.py:30
  178.1 9.0 %collective-permute-start.36 = (bf16[128,768]{1,0:T(8,128)(2,1)S(1)}, bf16[128,768]{1,0:T(8,128)(2,1)S(1)}, u32[]{:S(2)}, u32[]{:S(2)}) collective-permute-start(bf16[128,768]{1,0:T(8,128)(2,1)S(1)} %get-tuple-element.51), channel_id=1, source_target_pairs={{0,48},{8,200},{16,0},{24,216},{32,16},{40,232},{48,32},{56,248},{... | collective-permute-start | bytes 589832 | tf_op jit(solution)/shard_map/ppermute | solution.py:30
  188.6 8.8 %collective-permute-start.38 = (bf16[2,32,768]{2,1,0:T(8,128)(2,1)S(1)}, bf16[2,32,768]{2,1,0:T(8,128)(2,1)S(1)}, u32[]{:S(2)}, u32[]{:S(2)}) collective-permute-start(bf16[2,32,768]{2,1,0:T(8,128)(2,1)S(1)} %pad_maximum_fusion.3), channel_id=1, source_target_pairs={{0,7},{1,2},{2,1},{3,4},{4,3},{5,6},{6,5},{7,0},{8,15},{9,10},{10,... | collective-permute-start | bytes 294920 | tf_op jit(solution)/shard_map/ppermute | solution.py:38
  197.5 8.1 %collective-permute-start.39 = (bf16[2,32,768]{2,1,0:T(8,128)(2,1)S(1)}, bf16[2,32,768]{2,1,0:T(8,128)(2,1)S(1)}, u32[]{:S(2)}, u32[]{:S(2)}) collective-permute-start(bf16[2,32,768]{2,1,0:T(8,128)(2,1)S(1)} %add_convert_fusion.7), channel_id=1, source_target_pairs={{0,3},{1,6},{2,5},{3,0},{4,7},{5,2},{6,1},{7,4},{8,11},{9,14},{10,... | collective-permute-start | bytes 294920 | tf_op jit(solution)/shard_map/ppermute | solution.py:42
  (35 other events, 246.3 us)
